TPU v7x, 32 devices: a whole 2x2x4 slice. The times are simulated.
32 devices in a mesh: dp: 8 (over z, x), fsdp: 4 (over y, core).
Axes of the slice: x: 2, y: 2, z: 4, core: 2. Of those that a mesh axis runs over, the one named last changes fastest.
Arguments:
- tokens: bfloat16 [32, 2048, 512], P(('dp', 'fsdp')), may hold values from -6 to 6
- cotangent: bfloat16 [32, 2048, 512], P(('dp', 'fsdp')), may hold values from -6 to 6
- known_genes: int32 [32, 2048], P(('dp', 'fsdp')), may hold values 0 or 1
- cell_kind: int32 [32], P(('dp', 'fsdp')), may hold values from 0 to 1, as said below
- gene_counts: int32 [32, 4], P(('dp', 'fsdp')), may hold values from 0 to 2048, as said below
- study_index: int32 [32, 4], P(('dp', 'fsdp')), may hold values from 0 to 7, as said below
- qkv_weight: float32 [512, 1536], P('fsdp'), may hold values from -0.25 to 0.25
- qkv_first: float32 [512, 1536], P('fsdp'), may hold values from -1536 to 1536
- qkv_second: float32 [512, 1536], P('fsdp'), may hold values from 65536 to 262144
- proj_weight: float32 [512, 512], P('fsdp'), may hold values from -6 to 6
- proj_first: float32 [512, 512], P('fsdp'), may hold values from -128 to 128
- proj_second: float32 [512, 512], P('fsdp'), may hold values from 512 to 2048
- up_weight: float32 [512, 512], P('fsdp'), may hold values from -0.25 to 0.25
- up_first: float32 [512, 512], P('fsdp'), may hold values from -1536 to 1536
- up_second: float32 [512, 512], P('fsdp'), may hold values from 65536 to 262144
- down_weight: float32 [512, 512], P('fsdp'), may hold values from -0.25 to 0.25
- down_first: float32 [512, 512], P('fsdp'), may hold values from -768 to 768
- down_second: float32 [512, 512], P('fsdp'), may hold values from 16384 to 65536
- norm_params: float32 [4, 512], P(None, 'fsdp'), may hold values from -0.5 to 1.4, as said below
- norm_first: float32 [4, 512], P(None, 'fsdp'), may hold values from -1536 to 1536
- norm_second: float32 [4, 512], P(None, 'fsdp'), may hold values from 65536 to 262144
Outputs:
- out: bfloat16 [32, 2048, 512], P(('dp', 'fsdp'))
- input_grad: bfloat16 [32, 2048, 512], P(('dp', 'fsdp'))
- study_mean: float32 [8, 512], replicated
- study_var: float32 [8, 512], replicated
- qkv_first_new: float32 [512, 1536], P('fsdp')
- qkv_second_new: float32 [512, 1536], P('fsdp')
- qkv_weight_new: float32 [512, 1536], P('fsdp')
- qkv_weight_copy: bfloat16 [512, 1536], P('fsdp')
- proj_first_new: float32 [512, 512], P('fsdp')
- proj_second_new: float32 [512, 512], P('fsdp')
- proj_weight_new: float32 [512, 512], P('fsdp')
- proj_weight_copy: bfloat16 [512, 512], P('fsdp')
- up_first_new: float32 [512, 512], P('fsdp')
- up_second_new: float32 [512, 512], P('fsdp')
- up_weight_new: float32 [512, 512], P('fsdp')
- up_weight_copy: bfloat16 [512, 512], P('fsdp')
- down_first_new: float32 [512, 512], P('fsdp')
- down_second_new: float32 [512, 512], P('fsdp')
- down_weight_new: float32 [512, 512], P('fsdp')
- down_weight_copy: bfloat16 [512, 512], P('fsdp')
- norm_first_new: float32 [4, 512], P(None, 'fsdp')
- norm_second_new: float32 [4, 512], P(None, 'fsdp')
- norm_params_new: float32 [4, 512], P(None, 'fsdp')
- norm_params_copy: bfloat16 [4, 512], P(None, 'fsdp')
- matrix_norms: float32 [3, 4], replicated
Inputs may be any that keep to these rules, and one draw needn't show every extreme that they name: `cell_kind`: both kinds occur in every draw. `gene_counts`: slots 1 and up of a group with cell_kind 1 hold 0. A long cell has 1024 genes or more, some long cell exactly 2048; a short cell has 256 or more, some short cell exactly 512. `study_index`: every study has a used cell slot. `norm_params`: rows 0 and 2 are gains, rows 1 and 3 biases.
All inputs are finite; a program needn't handle non-finite values. No bound on the sum of `known_genes` on one device may be relied on, other than what follows from the above.
Results may differ from a plain program's by a relative error of at most 0.019.
Values may be sent and summed in bfloat16 or wider, within the bound.
No kernel may reach another device: no remote copies, remote signals or barrier semaphores. Data moves between devices by JAX's collectives and lax.ppermute only.
A program may use at most 256 MiB of HBM per device.

v0:
```python
from functools import partial

import jax
import jax.numpy as jnp
from jax import lax
from jax.experimental import pallas as pl
from jax.experimental.pallas import tpu as pltpu
from jax.sharding import PartitionSpec as P

HEADS = 8
HDIM = 64
SHORT_LENGTH = 512
STUDY_COUNT = 8
STEP = 5
PAIR = 2 * HDIM
PAIRS = HEADS // 2
KEY_BLOCK = 256
TAIL = 128


BETA = 0.5
ADAM_EPS = 1e-06
NORM_EPS = 1e-05
MATRIX_RATE = 0.5
VECTOR_RATE = 0.3
MATRIX_DECAY = 0.01
MASKED = -1000000000.0
SAFE_SCORE = 40.0

BF = jnp.bfloat16
F32 = jnp.float32
NN = (((1,), (0,)), ((), ()))
NT = (((1,), (1,)), ((), ()))
TN = (((0,), (0,)), ((), ()))
SMEM = pl.BlockSpec(memory_space=pltpu.SMEM)
ANY = pl.BlockSpec(memory_space=pl.ANY)


def mm(left, right, dims):
    return lax.dot_general(left, right, dims, preferred_element_type=F32)


def whole(*shape):
    return pl.BlockSpec(shape, lambda *_: (0,) * len(shape))


def params(mebibytes):
    return pltpu.CompilerParams(vmem_limit_bytes=mebibytes * 2**20)


def cost(flops, nbytes, trans=0):
    return pl.CostEstimate(flops=int(flops), bytes_accessed=int(nbytes), transcendentals=int(trans))


def iota(shape, dim):
    return lax.broadcasted_iota(jnp.int32, shape, dim)


def prep_kernel(kind, counts, known, tokens, cot, tokens_t, cot_t, packed, slot, meta):
    length = tokens.shape[0]
    cells = length // SHORT_LENGTH
    is_long = kind[0] == 1
    shape = (8, SHORT_LENGTH)
    row = iota(shape, 0)
    col = iota(shape, 1)
    given = jnp.zeros(shape, jnp.int32)
    for cell in range(cells):
        given = jnp.where(row == cell, known[0:1, pl.ds(cell * SHORT_LENGTH, SHORT_LENGTH)], given)
    limit = jnp.zeros(shape, jnp.int32)
    for cell in range(cells):
        limit = jnp.where(row == cell, counts[cell], limit)
    limit = jnp.where(is_long, counts[0] - SHORT_LENGTH * row, limit)
    first = (col == 0) & (jnp.logical_not(is_long) | (row == 0))
    usable = (col < limit) & ((given == 1) | first) & (row < cells)
    usable_f = jnp.where(usable, 1.0, 0.0)
    square = (SHORT_LENGTH, SHORT_LENGTH)
    before = jnp.where(iota(square, 0) < iota(square, 1), 1.0, 0.0).astype(BF)
    rank = mm(usable_f.astype(BF), before, NN).astype(jnp.int32)
    totals = [jnp.sum(usable_f[cell : cell + 1, :]).astype(jnp.int32) for cell in range(cells)]
    base = jnp.zeros(shape, jnp.int32)
    running = jnp.int32(0)
    for cell in range(cells):
        start = jnp.where(is_long, running, SHORT_LENGTH * cell)
        base = jnp.where(row == cell, start, base)
        running = running + totals[cell]
    place = jnp.where(usable, rank + base, -1)
    for cell in range(cells):
        slot[0:1, pl.ds(cell * SHORT_LENGTH, SHORT_LENGTH)] = place[cell : cell + 1, :]
    meta[0] = kind[0]
    for cell in range(cells):
        meta[1 + cell] = jnp.where(is_long, running if cell == 0 else 0, totals[cell])

    for block in range(length // KEY_BLOCK):
        rows = pl.ds(block * KEY_BLOCK, KEY_BLOCK)
        tokens_t[:, rows] = tokens[rows, :].T
        cot_t[:, rows] = cot[rows, :].T
        cell = block * KEY_BLOCK // SHORT_LENGTH
        inside = block * KEY_BLOCK - cell * SHORT_LENGTH
        needed = jnp.where(is_long, block * KEY_BLOCK < running, inside < totals[cell])

        @pl.when(needed)
        def _(block=block, rows=rows):
            hot = one_hot(slot, block * KEY_BLOCK, KEY_BLOCK)
            packed[rows, :] = mm(hot, tokens[...], NN).astype(BF)


def one_hot(slot, begin, rows):
    shape = (rows, slot.shape[1])
    hit = (iota(shape, 0) + begin) == slot[0:1, :]
    return jnp.where(hit, 1.0, 0.0).astype(BF)


def prep(kind, counts, known, tokens, cot):
    length, width = tokens.shape
    return pl.pallas_call(
        prep_kernel,
        in_specs=[SMEM, SMEM, whole(1, length), whole(length, width), whole(length, width)],
        out_specs=[
            whole(width, length),
            whole(width, length),
            whole(length, width),
            whole(1, length),
            SMEM,
        ],
        out_shape=[
            jax.ShapeDtypeStruct((width, length), BF),
            jax.ShapeDtypeStruct((width, length), BF),
            jax.ShapeDtypeStruct((length, width), BF),
            jax.ShapeDtypeStruct((1, length), jnp.int32),
            jax.ShapeDtypeStruct((8,), jnp.int32),
        ],
        compiler_params=params(56),
        cost_estimate=cost(3e9, 12e6),
        name="prep",
    )(kind, counts, known, tokens, cot)


def fetch_rows(pieces, mine, target, sem, kinds=1):
    rows = pieces[0].shape[0]
    copies = []
    for index, piece in enumerate(pieces):
        owner = jnp.bitwise_xor(mine, index)
        place = pl.ds(pl.multiple_of(owner * rows, rows), rows)
        if kinds == 1:
            copies.append((piece, target.at[place, :]))
            continue
        for pair in range(PAIRS):
            for kind in range(kinds):
                come = piece.at[:, pl.ds(PAIR * (PAIRS * kind + pair), PAIR)]
                copies.append((come, target.at[place, pl.ds(PAIR * (kinds * pair + kind), PAIR)]))
    copies = [pltpu.make_async_copy(*ends, sem.at[index]) for index, ends in enumerate(copies)]
    for copy in copies:
        copy.start()
    for copy in copies:
        copy.wait()


def head_lanes(shape, head):
    lane = iota(shape, 1)
    return (lane >= HDIM * head) & (lane < HDIM * (head + 1))


def spare(head):
    return HDIM * (1 - head)


def key_side(block, head, begin, count):
    lane = iota(block.shape, 1) - spare(head)
    row = iota(block.shape, 0) + begin
    bias = jnp.where(row < count, 0.0, MASKED)
    extra = jnp.where(lane == 0, bias, jnp.where((lane > 0) & (lane < 4), 1.0, 0.0))
    return jnp.where(head_lanes(block.shape, head), block.astype(F32), extra).astype(BF)


def value_side(block, head):
    lane = iota(block.shape, 1) - spare(head)
    extra = jnp.where((lane > 0) & (lane < 4), 1.0, 0.0)
    return jnp.where(head_lanes(block.shape, head), block.astype(F32), extra).astype(BF)


def split_rows(shift):
    high = shift.astype(BF).astype(F32)
    rest = shift - high
    mid = rest.astype(BF).astype(F32)
    low = rest - mid
    shape = (16, shift.shape[1])
    row = iota(shape, 0)
    out = jnp.where(row == 0, 1.0, 0.0)
    out = jnp.where(row == 1, -high, out)
    out = jnp.where(row == 2, -mid, out)
    return jnp.where(row == 3, -low, out).astype(BF)


def query_side(target, head, rows, shift):
    other = spare(head)
    target[head, HDIM * head : HDIM * (head + 1), :] = rows
    target[head, other : other + 16, :] = split_rows(shift)
    target[head, other + 16 : other + HDIM, :] = jnp.zeros((HDIM - 16, rows.shape[1]), BF)


def walk(meta, length, body):
    @pl.when(meta[0] == 1)
    def _():
        cell_walk(meta[1], 0, 0, length, body)

    @pl.when(meta[0] != 1)
    def _():
        for cell in range(length // SHORT_LENGTH):
            cell_walk(meta[1 + cell], cell * SHORT_LENGTH, cell * SHORT_LENGTH, SHORT_LENGTH, body)


def cell_walk(count, slot_begin, query_begin, queries, body):
    rest = lax.rem(count, KEY_BLOCK)
    tail = (rest > 0) & (rest <= TAIL)
    full = count // KEY_BLOCK + jnp.where(rest > TAIL, 1, 0)
    end = slot_begin + count

    @pl.loop(0, full)
    def _(index):
        begin = pl.multiple_of(slot_begin + index * KEY_BLOCK, KEY_BLOCK)
        body(begin, KEY_BLOCK, query_begin, queries, end)

    @pl.when(tail)
    def _():
        begin = pl.multiple_of(slot_begin + full * KEY_BLOCK, KEY_BLOCK)
        body(begin, TAIL, query_begin, queries, end)


def forward_kernel(count, mine, meta, *refs):
    pieces = refs[:count]
    tokens_t, packed, slot = refs[count : count + 3]
    q_out, k_out, v_out, kc_out, vc_out, kct_out, context, log_total = refs[count + 3 : count + 11]
    weights, vct, side, total, shift, sem = refs[count + 11 :]
    step = pl.program_id(0)
    length = tokens_t.shape[1]

    @pl.when(step == 0)
    def _():
        fetch_rows(pieces, mine[0], weights, sem, 3)

    columns = pl.ds(pl.multiple_of(step * 3 * PAIR, 3 * PAIR), 3 * PAIR)
    part = weights[:, columns]
    joined = mm(part, tokens_t[...], TN)
    q_out[...] = (joined[:PAIR] * HDIM**-0.5).astype(BF)
    k_out[...] = joined[PAIR : 2 * PAIR].astype(BF)
    v_out[...] = joined[2 * PAIR :].astype(BF)

    def project(begin, rows, *_):
        place = pl.ds(begin, rows)
        both = mm(packed[place, :], part[:, PAIR:], NN).astype(BF)
        kc_out[place, :] = both[:, :PAIR]
        vc_out[place, :] = both[:, PAIR:]
        kct_out[:, place] = both[:, :PAIR].T
        turned = both[:, PAIR:].T
        ones = jnp.where(iota((16, rows), 0) == 0, 1.0, 0.0).astype(BF)
        for head in range(2):
            vct[head, :HDIM, place] = turned[HDIM * head : HDIM * (head + 1)]
            vct[head, HDIM:, place] = ones

    walk(meta, length, project)

    masked = slot[...] < 0
    own = []
    for head in range(2):
        rows = slice(HDIM * head, HDIM * (head + 1))
        queries = q_out[rows, :].astype(F32)
        keys = k_out[rows, :].astype(F32)
        own.append(jnp.where(masked, jnp.sum(queries * keys, axis=0, keepdims=True), MASKED))
        top_q = jnp.max(jnp.sum(queries * queries, axis=0, keepdims=True))
        top_k = jnp.max(jnp.sum(keys * keys, axis=0, keepdims=True))
        unsafe = jnp.logical_not(top_q * top_k < SAFE_SCORE * SAFE_SCORE)
        shift[head : head + 1, :] = jnp.zeros((1, length), F32)
        query_side(side, head, q_out[rows, :], jnp.zeros((1, length), F32))

        @pl.when(unsafe)
        def _(head=head, rows=rows):
            shift[head : head + 1, :] = own[head]

            def raise_top(begin, rows, first, queries, end):
                keys = key_side(kc_out[pl.ds(begin, rows), :], head, begin, end)
                place = pl.ds(first, queries)
                scores = mm(keys, side[head, :, place], NN)
                top = jnp.max(scores, axis=0, keepdims=True)
                shift[head : head + 1, place] = jnp.maximum(shift[head : head + 1, place], top)

            walk(meta, length, raise_top)
            query_side(side, head, q_out[rows, :], shift[head : head + 1, :])

    total[...] = jnp.zeros(total.shape, F32)

    def attend(begin, rows, first, queries, end):
        slots = pl.ds(begin, rows)
        place = pl.ds(first, queries)
        for head in range(2):
            keys = key_side(kc_out[slots, :], head, begin, end)
            raised = jnp.exp(mm(keys, side[head, :, place], NN)).astype(BF)
            total[head, :, place] += mm(vct[head, :, slots], raised, NN)

    walk(meta, length, attend)

    for head in range(2):
        rows = slice(HDIM * head, HDIM * (head + 1))
        alone = jnp.exp(own[head] - shift[head : head + 1, :])
        row_total = total[head, HDIM : HDIM + 1, :] + alone
        gathered = total[head, :HDIM, :] + v_out[rows, :].astype(F32) * alone
        context[rows, :] = (gathered / row_total).astype(BF)
        log_total[pl.ds(step * 2 + head, 1), :] = shift[head : head + 1, :] + jnp.log(row_total)


def forward(mine, meta, pieces, tokens_t, packed, slot):
    width, length = tokens_t.shape
    pair_rows = pl.BlockSpec((PAIR, length), lambda step: (step, 0))
    pair_lanes = pl.BlockSpec((length, PAIR), lambda step: (0, step))
    transposed = jax.ShapeDtypeStruct((width, length), BF)
    natural = jax.ShapeDtypeStruct((length, width), BF)
    count = len(pieces)
    return pl.pallas_call(
        partial(forward_kernel, count),
        grid=(PAIRS,),
        in_specs=[SMEM, SMEM]
        + [ANY] * count
        + [whole(width, length), whole(length, width), whole(1, length)],
        out_specs=[pair_rows] * 3 + [pair_lanes] * 2 + [pair_rows] * 2 + [whole(HEADS, length)],
        out_shape=[transposed] * 3
        + [natural] * 2
        + [transposed] * 2
        + [jax.ShapeDtypeStruct((HEADS, length), F32)],
        scratch_shapes=[
            pltpu.VMEM((width, 3 * width), BF),
            pltpu.VMEM((2, HDIM + 16, length), BF),
            pltpu.VMEM((2, PAIR, length), BF),
            pltpu.VMEM((2, HDIM + 16, length), F32),
            pltpu.VMEM((8, length), F32),
            pltpu.SemaphoreType.DMA((3 * PAIRS * count,)),
        ],
        compiler_params=params(56),
        cost_estimate=cost(15e9, 25e6, 20e6),
        name="attend_forward",
    )(mine, meta, *pieces, tokens_t, packed, slot)


def backward_kernel(pair, meta, *refs):
    q_t, k_t, v_t, kc, vc, kct, grad_context, log_total, inner, slot, tokens_t = refs[:11]
    grad_t, grad_weight = refs[11:13]
    q_side, g_side, grad_q, grad_kv, ready = refs[13:]
    length = tokens_t.shape[1]
    for head in range(2):
        rows = slice(HDIM * head, HDIM * (head + 1))
        index = 2 * pair + head
        query_side(q_side, head, q_t[rows, :], log_total[index : index + 1, :])
        query_side(g_side, head, grad_context[rows, :], inner[index : index + 1, :])
    grad_q[...] = jnp.zeros(grad_q.shape, F32)
    grad_kv[...] = jnp.zeros(grad_kv.shape, F32)

    def pull(begin, rows, first, queries, end):
        slots = pl.ds(begin, rows)
        place = pl.ds(first, queries)
        for head in range(2):
            lanes = slice(HDIM * head, HDIM * (head + 1))
            keys = key_side(kc[slots, :], head, begin, end)
            values = value_side(vc[slots, :], head)
            probs = jnp.exp(mm(keys, q_side[head, :, place], NN))
            grad_scores = (probs * mm(values, g_side[head, :, place], NN)).astype(BF)
            grad_q[lanes, place] += mm(kct[lanes, slots], grad_scores, NN)
            ready[HDIM * head : HDIM * (head + 1), :rows] = mm(
                q_t[lanes, place], grad_scores, NT
            ).astype(BF)
            ready[PAIR + HDIM * head : PAIR + HDIM * (head + 1), :rows] = mm(
                grad_context[lanes, place], probs.astype(BF), NT
            ).astype(BF)
        hit = (iota((rows, queries), 0) + begin) == slot[0:1, place]
        spread = jnp.where(hit, 1.0, 0.0).astype(BF)
        grad_kv[:, place] += mm(ready[:, :rows], spread, NN)

    walk(meta, length, pull)

    masked = slot[...] < 0
    for head in range(2):
        rows = slice(HDIM * head, HDIM * (head + 1))
        index = 2 * pair + head
        queries = q_t[rows, :].astype(F32)
        keys = k_t[rows, :].astype(F32)
        values = v_t[rows, :].astype(F32)
        grads = grad_context[rows, :].astype(F32)
        own = jnp.sum(queries * keys, axis=0, keepdims=True)
        own = jnp.where(masked, own - log_total[index : index + 1, :], MASKED)
        alone = jnp.exp(own)
        pulled = jnp.sum(grads * values, axis=0, keepdims=True) - inner[index : index + 1, :]
        pulled = (alone * pulled).astype(BF).astype(F32)
        alone = alone.astype(BF).astype(F32)
        part = (grad_q[rows, :] + keys * pulled) * HDIM**-0.5
        grad_t[HDIM * head : HDIM * (head + 1), :] = part.astype(BF)
        part = grad_kv[rows, :] + queries * pulled
        grad_t[PAIR + HDIM * head : PAIR + HDIM * (head + 1), :] = part.astype(BF)
        part = grad_kv[PAIR + HDIM * head : PAIR + HDIM * (head + 1), :] + grads * alone
        grad_t[2 * PAIR + HDIM * head : 2 * PAIR + HDIM * (head + 1), :] = part.astype(BF)
    grad_weight[...] = mm(tokens_t[...], grad_t[...], NT).astype(BF)


def backward(pair, meta, q_t, k_t, v_t, kc, vc, kct, grad_context, log_total, inner, slot, tokens_t):
    width, length = tokens_t.shape
    pair_rows = pl.BlockSpec((PAIR, length), lambda step: (pair, 0))
    pair_lanes = pl.BlockSpec((length, PAIR), lambda step: (0, pair))
    return pl.pallas_call(
        partial(backward_kernel, pair),
        grid=(1,),
        in_specs=[SMEM]
        + [pair_rows] * 3
        + [pair_lanes] * 2
        + [pair_rows] * 2
        + [whole(HEADS, length)] * 2
        + [whole(1, length), whole(width, length)],
        out_specs=[whole(3 * PAIR, length), whole(width, 3 * PAIR)],
        out_shape=[
            jax.ShapeDtypeStruct((3 * PAIR, length), BF),
            jax.ShapeDtypeStruct((width, 3 * PAIR), BF),
        ],
        scratch_shapes=[
            pltpu.VMEM((2, PAIR, length), BF),
            pltpu.VMEM((2, PAIR, length), BF),
            pltpu.VMEM((PAIR, length), F32),
            pltpu.VMEM((2 * PAIR, length), F32),
            pltpu.VMEM((2 * PAIR, KEY_BLOCK), BF),
        ],
        compiler_params=params(56),
        cost_estimate=cost(12e9, 10e6, 6e6),
        name=f"attend_backward_{pair}",
    )(meta, q_t, k_t, v_t, kc, vc, kct, grad_context, log_total, inner, slot, tokens_t)


def feature_mean(values):
    return jnp.sum(values, axis=0, keepdims=True) * (1.0 / values.shape[0])


def normalise(values):
    centred = values - feature_mean(values)
    scale = lax.rsqrt(feature_mean(centred * centred) + NORM_EPS)
    return centred * scale, scale


def pull_norm(grad, scaled, scale, gain):
    lifted = grad * gain
    return scale * (lifted - feature_mean(lifted) - scaled * feature_mean(lifted * scaled))


def lane_sums(values):
    width = 128
    out = values[:, :width]
    for begin in range(width, values.shape[1], width):
        out = out + values[:, begin : begin + width]
    return out


def dense_kernel(count, mine, *refs):
    pieces = refs[:count]
    tokens_t, context, cot_t = refs[count : count + 3]
    out, grad_context, grad_first, inner, g_proj, g_up, g_down, g_norm = refs[count + 3 : count + 11]
    weights, total, norm_total, sem = refs[count + 11 :]
    step = pl.program_id(0)
    width = tokens_t.shape[0]

    @pl.when(step == 0)
    def _():
        fetch_rows(pieces, mine[0], weights, sem)
        total[...] = jnp.zeros(total.shape, F32)
        norm_total[...] = jnp.zeros(norm_total.shape, F32)

    proj = weights[:, :width]
    up = weights[:, width : 2 * width]
    down = weights[:, 2 * width : 3 * width]
    rows = weights[:, 3 * width :].astype(F32)
    gain1, bias1, gain2, bias2 = (rows[:, index : index + 1] for index in range(4))

    context_low = context[...]
    scaled1, scale1 = normalise(tokens_t[...].astype(F32) + mm(proj, context_low, TN))
    middle = scaled1 * gain1 + bias1
    middle_low = middle.astype(BF)
    hidden = mm(up, middle_low, TN)
    cdf = 0.5 * (1.0 + lax.erf(hidden * 2.0**-0.5))
    slope = cdf + hidden * jnp.exp(hidden * hidden * -0.5) * 0.3989422804014327
    active = (hidden * cdf).astype(BF)
    scaled2, scale2 = normalise(middle + mm(down, active, TN))
    out[...] = (scaled2 * gain2 + bias2).astype(BF).T

    cot = cot_t[...].astype(F32)
    norm_total[2] += lane_sums(cot * scaled2)
    norm_total[3] += lane_sums(cot)
    grad_second = pull_norm(cot, scaled2, scale2, gain2)
    grad_low = grad_second.astype(BF)
    total[2] += mm(active, grad_low, NT)
    grad_hidden = (mm(down, grad_low, NN) * slope).astype(BF)
    total[1] += mm(middle_low, grad_hidden, NT)
    grad_middle = grad_second + mm(up, grad_hidden, NN)
    norm_total[0] += lane_sums(grad_middle * scaled1)
    norm_total[1] += lane_sums(grad_middle)
    grad_h1 = pull_norm(grad_middle, scaled1, scale1, gain1)
    grad_first[...] = grad_h1
    proj_low = grad_h1.astype(BF)
    total[0] += mm(context_low, proj_low, NT)
    pulled = mm(proj, proj_low, NN).astype(BF)
    grad_context[...] = pulled
    both = pulled.astype(F32) * context_low.astype(F32)
    for head in range(HEADS):
        part = both[HDIM * head : HDIM * (head + 1), :]
        inner[head : head + 1, :] = jnp.sum(part, axis=0, keepdims=True)

    @pl.when(step == pl.num_programs(0) - 1)
    def _():
        g_proj[...] = total[0].astype(BF)
        g_up[...] = total[1].astype(BF)
        g_down[...] = total[2].astype(BF)
        lane = iota((width, 128), 1)
        packed = jnp.zeros((width, 128), F32)
        for index in range(4):
            column = jnp.sum(norm_total[index], axis=1, keepdims=True)
            packed = jnp.where(lane == index, column, packed)
        g_norm[...] = packed


def dense(mine, pieces, tokens_t, context, cot_t):
    width, length = tokens_t.shape
    block = 512
    count = len(pieces)
    columns = pl.BlockSpec((width, block), lambda step: (0, step))
    square = jax.ShapeDtypeStruct((width, width), BF)
    return pl.pallas_call(
        partial(dense_kernel, count),
        grid=(length // block,),
        in_specs=[SMEM] + [ANY] * count + [columns] * 3,
        out_specs=[
            pl.BlockSpec((block, width), lambda step: (step, 0)),
            columns,
            columns,
            pl.BlockSpec((HEADS, block), lambda step: (0, step)),
        ]
        + [whole(width, width)] * 3
        + [whole(width, 128)],
        out_shape=[
            jax.ShapeDtypeStruct((length, width), BF),
            jax.ShapeDtypeStruct((width, length), BF),
            jax.ShapeDtypeStruct((width, length), F32),
            jax.ShapeDtypeStruct((HEADS, length), F32),
        ]
        + [square] * 3
        + [jax.ShapeDtypeStruct((width, 128), F32)],
        scratch_shapes=[
            pltpu.VMEM((width, 3 * width + 128), BF),
            pltpu.VMEM((3, width, width), F32),
            pltpu.VMEM((4, width, 128), F32),
            pltpu.SemaphoreType.DMA((count,)),
        ],
        compiler_params=params(56),
        cost_estimate=cost(10e9, 20e6, 4e6),
        name="dense",
    )(mine, *pieces, tokens_t, context, cot_t)


def input_kernel(count, mine, *refs):
    pieces = refs[:count]
    grads = refs[count : count + PAIRS]
    grad_first, out = refs[count + PAIRS : count + PAIRS + 2]
    weights, sem = refs[count + PAIRS + 2 :]

    @pl.when(pl.program_id(0) == 0)
    def _():
        fetch_rows(pieces, mine[0], weights, sem, 3)

    total = grad_first[...]
    for pair in range(PAIRS):
        total = total + mm(weights[:, 3 * PAIR * pair : 3 * PAIR * (pair + 1)], grads[pair][...], NN)
    out[...] = total.astype(BF).T


def input_side(mine, pieces, grads, grad_first):
    width, length = grad_first.shape
    block = 512
    count = len(pieces)
    return pl.pallas_call(
        partial(input_kernel, count),
        grid=(length // block,),
        in_specs=[SMEM]
        + [ANY] * count
        + [pl.BlockSpec((3 * PAIR, block), lambda step: (0, step))] * PAIRS
        + [pl.BlockSpec((width, block), lambda step: (0, step))],
        out_specs=pl.BlockSpec((block, width), lambda step: (step, 0)),
        out_shape=jax.ShapeDtypeStruct((length, width), BF),
        scratch_shapes=[
            pltpu.VMEM((width, 3 * width), BF),
            pltpu.SemaphoreType.DMA((3 * PAIRS * count,)),
        ],
        compiler_params=params(56),
        cost_estimate=cost(3.3e9, 14e6),
        name="input_side",
    )(mine, *pieces, *grads, grad_first)


def swap(value, axis, size, mask):
    return lax.ppermute(value, axis, [(index, index ^ mask) for index in range(size)])


def masks_of(size):
    return [1 << bit for bit in range(size.bit_length() - 1)]


def gather_pieces(piece, axis, size, meanwhile):
    pieces = {0: piece}
    for mask in reversed(masks_of(size)):
        for known in list(pieces):
            pieces[known ^ mask] = swap(pieces[known], axis, size, mask)
            if meanwhile is not None:
                meanwhile, pieces[mask] = lax.optimization_barrier((meanwhile, pieces[mask]))
                meanwhile = None
    return [pieces[index] for index in range(size)]


def halving(value, axis, size):
    mine = lax.axis_index(axis)
    rows = value.shape[0] // size
    value = value.reshape(size, rows, -1)
    for bit, mask in enumerate(masks_of(size)):
        value = value.reshape(value.shape[0] // 2, 2, rows, -1).swapaxes(0, 1)
        side = (mine >> bit) & 1
        send = lax.dynamic_index_in_dim(value, 1 - side, 0, keepdims=False)
        got = yield send, axis, size, mask
        keep = lax.dynamic_index_in_dim(value, side, 0, keepdims=False)
        value = (keep.astype(F32) + got.astype(F32)).astype(value.dtype)
    return value.reshape(rows, -1)


def doubling(value, axis, size):
    for mask in masks_of(size):
        got = yield value, axis, size, mask
        value = (value.astype(F32) + got.astype(F32)).astype(value.dtype)
    return value


def side_steps(value, fsdp, dp):
    value = yield from halving(value, "fsdp", fsdp)
    return (yield from doubling(value, "dp", dp))


def small_steps(value, fsdp, dp):
    value = yield from doubling(value, "fsdp", fsdp)
    return (yield from doubling(value, "dp", dp))


class Chain:
    def __init__(self, steps):
        self.steps, self.result, self.got = steps, None, None
        self.request = next(steps)

    def send(self, value):
        _, axis, size, mask = self.request
        self.got = swap(value, axis, size, mask)

    def land(self, value):
        try:
            self.request = self.steps.send(value)
        except StopIteration as end:
            self.request, self.result = None, end.value

    def finish(self):
        while self.request is not None:
            if self.got is None:
                self.send(self.request[0])
            value, self.got = self.got, None
            self.land(value)
        return self.result


def start_steps(anchor, chains):
    live = [chain for chain in chains if chain.request is not None]
    anchor, *values = lax.optimization_barrier((anchor, *(chain.request[0] for chain in live)))
    for chain, value in zip(live, values):
        chain.send(value)
    return anchor


def end_steps(anchor, chains):
    live = [chain for chain in chains if chain.got is not None]
    anchor, *values = lax.optimization_barrier((anchor, *(chain.got for chain in live)))
    for chain, value in zip(live, values):
        chain.got = None
        chain.land(value)
    return anchor


def total_by_exchange(value, axis, size):
    rows, columns = value.shape
    parts = lax.all_to_all(value, axis, 0, 0, tiled=True).reshape(size, rows // size, columns)
    mine = jnp.sum(parts.astype(F32), axis=0).astype(BF)
    return lax.all_to_all(jnp.tile(mine, (size, 1)), axis, 0, 0, tiled=True)


def moments(gradient, first_old, second_old):
    first_new = BETA * first_old + (1.0 - BETA) * gradient
    second_new = BETA * second_old + (1.0 - BETA) * gradient * gradient
    return first_new, second_new


def update_of(first_new, second_new):
    debias = 1.0 - BETA**STEP
    return first_new / debias / (jnp.sqrt(second_new / debias) + ADAM_EPS)


def square_row(values):
    total = jnp.sum(values * values, axis=0, keepdims=True)
    return lane_sums(total)


def moments_kernel(count, paired, gradient, *refs):
    olds, outs, squares = refs[: 3 * count], refs[3 * count : 5 * count], refs[5 * count]
    at = 0
    squares[...] = jnp.zeros(squares.shape, F32)
    for index in range(count):
        weight, first_old, second_old = (ref[...] for ref in olds[3 * index : 3 * index + 3])
        columns = weight.shape[1]
        if paired:
            places = [
                3 * PAIR * (PAIRS - 1 - pair) + PAIR * kind
                for kind in range(3)
                for pair in range(PAIRS)
            ]
            grad = jnp.concatenate([gradient[:, at : at + PAIR] for at in places], axis=1)
        else:
            grad = gradient[:, at : at + columns]
        grad = grad.astype(F32)
        at += columns
        first_new, second_new = moments(grad, first_old, second_old)
        outs[2 * index][...] = first_new
        outs[2 * index + 1][...] = second_new
        update = update_of(first_new, second_new) + MATRIX_DECAY * weight
        squares[index : index + 1, :] = square_row(weight)
        squares[4 + index : 5 + index, :] = square_row(update)


def new_moments(gradient, olds, paired):
    shapes = [jax.ShapeDtypeStruct(old.shape, F32) for old in olds]
    count = len(olds) // 3
    outs = [shape for shape in shapes[::3] for _ in range(2)]
    results = pl.pallas_call(
        partial(moments_kernel, count, paired),
        out_shape=outs + [jax.ShapeDtypeStruct((8, 128), F32)],
        compiler_params=params(56),
        cost_estimate=cost(5e6, 5e6),
        name="moments",
    )(gradient, *olds)
    return results[:-1], results[-1]


def apply_kernel(count, squares, *refs):
    inputs, outs, norms = refs[: 3 * count], refs[3 * count : 5 * count], refs[5 * count]
    total = jnp.sum(jnp.sum(squares[...], axis=0), axis=1, keepdims=True)
    size = jnp.sqrt(total)
    ratio = size[0:4] / size[4:8]
    lane = iota((1, 4), 1)
    rows = [jnp.zeros((1, 4), F32)] * 3
    for index in range(count):
        weight, first_new, second_new = (ref[...] for ref in inputs[3 * index : 3 * index + 3])
        update = update_of(first_new, second_new) + MATRIX_DECAY * weight
        trust = ratio[index : index + 1]
        weight = weight - MATRIX_RATE * trust * update
        outs[2 * index][...] = weight
        outs[2 * index + 1][...] = weight.astype(BF)
        for place, value in enumerate((size[index : index + 1], size[4 + index : 5 + index], trust)):
            rows[place] = jnp.where(lane == index, value, rows[place])
    for place in range(3):
        norms[place : place + 1, :] = rows[place]


def apply_updates(squares, arrays):
    count = len(arrays) // 3
    outs = []
    for weight in arrays[::3]:
        outs += [jax.ShapeDtypeStruct(weight.shape, F32), jax.ShapeDtypeStruct(weight.shape, BF)]
    results = pl.pallas_call(
        partial(apply_kernel, count),
        out_shape=outs + [jax.ShapeDtypeStruct((3, 4), F32)],
        compiler_params=params(56),
        cost_estimate=cost(5e6, 8e6),
        name="apply",
    )(squares, *arrays)
    return results[:-1], results[-1]


def shards(
    fsdp,
    dp,
    tokens,
    cotangent,
    known_genes,
    cell_kind,
    gene_counts,
    study_index,
    qkv_weight,
    qkv_first,
    qkv_second,
    proj_weight,
    proj_first,
    proj_second,
    up_weight,
    up_first,
    up_second,
    down_weight,
    down_first,
    down_second,
    norm_params,
    norm_first,
    norm_second,
):
    _, length, width = tokens.shape
    mine = lax.axis_index("fsdp").astype(jnp.int32)
    mine_ref = mine.reshape(1)

    tokens_t, cot_t, packed, slot, meta = prep(
        cell_kind, gene_counts.reshape(-1), known_genes, tokens[0], cotangent[0]
    )
    qkv_pieces = gather_pieces(qkv_weight.astype(BF), "fsdp", fsdp, slot)
    norm_columns = jnp.pad(norm_params.T, ((0, 0), (0, 124)))
    rest = jnp.concatenate([proj_weight, up_weight, down_weight, norm_columns], axis=1).astype(BF)
    *qkv_pieces, rest, slot = lax.optimization_barrier((*qkv_pieces, rest, slot))
    q_t, k_t, v_t, kc, vc, kct, context, log_total = forward(
        mine_ref, meta, qkv_pieces, tokens_t, packed, slot
    )
    rest_pieces = gather_pieces(rest, "fsdp", fsdp, q_t)
    out, grad_context, grad_first, inner, g_proj, g_up, g_down, g_norm = dense(
        mine_ref, rest_pieces, tokens_t, context, cot_t
    )

    first_cells = out.reshape(-1, SHORT_LENGTH, width)[:, 0, :].astype(F32)
    slot_index = jnp.arange(first_cells.shape[0], dtype=jnp.int32)
    used_slots = (cell_kind[0] == 0) | (slot_index == 0)
    member = (
        (study_index[0][:, None] == jnp.arange(STUDY_COUNT, dtype=jnp.int32)[None, :])
        & used_slots[:, None]
    ).astype(F32)
    counts = jnp.broadcast_to(jnp.sum(member, axis=0)[:, None], (STUDY_COUNT, width))
    sums = jnp.sum(member[:, :, None] * first_cells[:, None, :], axis=0)
    squares = jnp.sum(member[:, :, None] * (first_cells * first_cells)[:, None, :], axis=0)
    small = jnp.concatenate([counts, sums, squares, g_norm[:, :8].T], axis=0)
    small_chain = Chain(small_steps(small, fsdp, dp))
    side_chain = Chain(side_steps(jnp.concatenate([g_proj, g_up, g_down], axis=1), fsdp, dp))
    chains = [side_chain, small_chain]
    half_chains = []
    grads = []
    parts = []
    for pair in reversed(range(PAIRS)):
        meta = start_steps(meta, chains)
        grad_t, part = backward(
            pair, meta, q_t, k_t, v_t, kc, vc, kct, grad_context, log_total, inner, slot, tokens_t
        )
        part = end_steps(part, chains)
        grads.append(grad_t)
        parts.append(part)
        if len(parts) * 2 == PAIRS:
            half_chains.append(Chain(halving(jnp.concatenate(parts, axis=1), "fsdp", fsdp)))
            chains.append(half_chains[-1])
            parts = []
    mine_ref = start_steps(mine_ref, chains)
    mine_ref = end_steps(mine_ref, half_chains)
    mine_ref = start_steps(mine_ref, half_chains)
    input_grad = input_side(mine_ref, qkv_pieces, grads[::-1], grad_first)
    input_grad = end_steps(input_grad, half_chains)
    qkv_share = jnp.concatenate([chain.finish() for chain in half_chains], axis=1)
    qkv_share = total_by_exchange(qkv_share, "dp", dp)
    qkv_share = end_steps(qkv_share, chains)
    side_share = side_chain.finish()
    small = small_chain.finish()
    study_mean = small[8:16] / small[:8]
    study_var = small[16:24] / small[:8] - study_mean * study_mean
    norm_share = lax.dynamic_slice_in_dim(small[24:28], mine * (width // fsdp), width // fsdp, 1)
    norm_first, norm_second = moments(norm_share, norm_first, norm_second)
    norm_params = norm_params - VECTOR_RATE * update_of(norm_first, norm_second)

    side_old = (proj_weight, proj_first, proj_second, up_weight, up_first, up_second)
    side_old += (down_weight, down_first, down_second)
    (qkv_first, qkv_second), qkv_squares = new_moments(
        qkv_share, (qkv_weight, qkv_first, qkv_second), True
    )
    side_new, side_squares = new_moments(side_share, side_old, False)
    squares = jnp.concatenate(
        [qkv_squares[0:1], side_squares[0:3], qkv_squares[4:5], side_squares[4:7]], axis=0
    )
    squares = lax.all_gather(squares, "fsdp", axis=0)
    arrays = (qkv_weight, qkv_first, qkv_second, proj_weight, side_new[0], side_new[1])
    arrays += (up_weight, side_new[2], side_new[3], down_weight, side_new[4], side_new[5])
    applied, matrix_norms = apply_updates(squares, arrays)
    results = []
    for index in range(4):
        results += [arrays[3 * index + 1], arrays[3 * index + 2]]
        results += [applied[2 * index], applied[2 * index + 1]]
    return (
        out.reshape(tokens.shape),
        input_grad.reshape(tokens.shape),
        study_mean,
        study_var,
        *results,
        norm_first,
        norm_second,
        norm_params,
        norm_params.astype(BF),
        matrix_norms,
    )


def solution(mesh):
    whole_groups = P(("dp", "fsdp"))
    rows = P("fsdp", None)
    columns = P(None, "fsdp")
    return jax.shard_map(
        partial(shards, mesh.shape["fsdp"], mesh.shape["dp"]),
        mesh=mesh,
        in_specs=(whole_groups,) * 6 + (rows,) * 12 + (columns,) * 3,
        out_specs=(whole_groups,) * 2 + (P(), P()) + (rows,) * 16 + (columns,) * 4 + (P(),),
        check_vma=False,
    )
```

profile of v0, /device:TPU:0, one launch (start us, length us, event | category | flops | bytes accessed | tf_op | source)
XLA Modules:
  0.0 280.9 jit_solution(11270200290591664368)
XLA Ops:
  1.9 3.0 %collective-permute-start.1 = (bf16[128,1536]{1,0:T(8,128)(2,1)S(1)}, bf16[128,1536]{1,0:T(8,128)(2,1)S(1)}, u32[]{:S(2)}, u32[]{:S(2)}) collective-permute-start(bf16[128,1536]{1,0:T(8,128)(2,1)S(1)} %convert_element_type.119.refs_0_), channel_id=1, source_target_pairs={{0,2},{1,3},{2,0},{3,1},{4,6},{5,7},{6,4},{7,5},{8,10},{9,11},{10,... | collective-permute-start | bytes 1179656 | tf_op jit(solution)/shard_map/ppermute | solution.py:598
  5.6 9.0 %prep.1 = (bf16[512,2048]{1,0:T(8,128)(2,1)}, bf16[512,2048]{1,0:T(8,128)(2,1)}, bf16[2048,512]{1,0:T(8,128)(2,1)}, s32[1,2048]{1,0:T(1,128)}, s32[8]{0:T(128)}) custom-call(s32[1]{0:T(128)S(6)} %copy.82.kind, s32[4]{0:T(128)} %bitcast.61, s32[1,2048]{1,0:T(1,128)} %known.1, bf16[2048,512]{1,0:T(8,128)(2,1)} %bitcast.59, bf16[2048,512]{1,0:T(8,128)(2,1)} %bitcast.60), custom_call_target="tpu_custom_call" | custom-call | flops 3000000000 | bytes 12000000 | tf_op jit(solution)/shard_map/prep/pallas_call | solution.py:115
  18.0 28.2 %attend_forward.1 = (bf16[512,2048]{1,0:T(8,128)(2,1)}, bf16[512,2048]{1,0:T(8,128)(2,1)}, bf16[512,2048]{1,0:T(8,128)(2,1)}, bf16[2048,512]{1,0:T(8,128)(2,1)},...) custom-call(s32[1]{0:T(128)} %bitcast.mine, ...), custom_call_target="tpu_custom_call" | custom-call | flops 15000000512 | bytes 25000000 | tf_op jit(solution)/shard_map/attend_forward/pallas_call | solution.py:317
  46.3 7.1 %collective-permute-start.5 = (bf16[128,1664]{1,0:T(8,128)(2,1)S(1)}, bf16[128,1664]{1,0:T(8,128)(2,1)S(1)}, u32[]{:S(2)}, u32[]{:S(2)}) collective-permute-start(bf16[128,1664]{1,0:T(8,128)(2,1)S(1)} %collective-permute-done.4.refs_2_), channel_id=1, source_target_pairs={{0,1},{1,0},{2,3},{3,2},{4,5},{5,4},{6,7},{7,6},{8,9},{9,8},{10,11... | collective-permute-start | bytes 1277960 | tf_op jit(solution)/shard_map/ppermute | solution.py:598
  55.5 25.4 %dense.1 = (bf16[2048,512]{1,0:T(8,128)(2,1)}, bf16[512,2048]{1,0:T(8,128)(2,1)}, f32[512,2048]{1,0:T(8,128)}, f32[8,2048]{1,0:T(8,128)}, bf16[512,512]{1,0:T(8,...) custom-call(s32[1]{0:T(128)} %bitcast.mine, bf16[128,1664]{1,0:T(8,128)(2,1)} %copy-done.5, ...), custom_call_target="tpu_custom_call" | custom-call | flops 10000000000 | bytes 20000000 | tf_op jit(solution)/shard_map/dense/pallas_call | solution.py:526
  85.8 14.6 %attend_backward_3.1 = (bf16[384,2048]{1,0:T(8,128)(2,1)}, bf16[512,384]{1,0:T(8,128)(2,1)}) custom-call(s32[8]{0:T(128)} %get-tuple-element.172.meta, bf16[512,2048]{1,0:T(8,128)(2,1)} %get-tuple-element.133.refs_0_, bf16[512,2048]{1,0:T(8,128)(2,1)} %get-tuple-element.143.refs_1_, bf16[512,2048]{1,0:T(8,128)(2,1)} %get-tuple-element.144.refs_2_, ...), custom_call_target="tpu_custom_call" | custom-call | flops 12000000000 | bytes 10000000 | tf_op jit(solution)/shard_map/attend_backward_3/pallas_call | solution.py:404
  100.7 4.9 %collective-permute-start.8 = (bf16[1,128,1536]{2,1,0:T(8,128)(2,1)S(1)}, bf16[1,128,1536]{2,1,0:T(8,128)(2,1)S(1)}, u32[]{:S(2)}, u32[]{:S(2)}) collective-permute-start(bf16[1,128,1536]{2,1,0:T(8,128)(2,1)S(1)} %constant_dynamic-slice_fusion.3), channel_id=1, source_target_pairs={{0,2},{1,3},{2,0},{3,1},{4,6},{5,7},{6,4},{7,5},{8,10},{9,11},{10,... | collective-permute-start | bytes 1179656 | tf_op jit(solution)/shard_map/ppermute | solution.py:598
  105.6 14.6 %attend_backward_2.1 = (bf16[384,2048]{1,0:T(8,128)(2,1)}, bf16[512,384]{1,0:T(8,128)(2,1)}) custom-call(s32[8]{0:T(128)} %get-tuple-element.172.meta, bf16[512,2048]{1,0:T(8,128)(2,1)} %get-tuple-element.133.refs_0_, bf16[512,2048]{1,0:T(8,128)(2,1)} %get-tuple-element.143.refs_1_, bf16[512,2048]{1,0:T(8,128)(2,1)} %get-tuple-element.144.refs_2_, ...), custom_call_target="tpu_custom_call" | custom-call | flops 12000000000 | bytes 10000000 | tf_op jit(solution)/shard_map/attend_backward_2/pallas_call | solution.py:404
  121.5 19.6 %collective-permute-start.10 = (bf16[128,1536]{1,0:T(8,128)(2,1)S(1)}, bf16[128,1536]{1,0:T(8,128)(2,1)S(1)}, u32[]{:S(2)}, u32[]{:S(2)}) collective-permute-start(bf16[128,1536]{1,0:T(8,128)(2,1)S(1)} %fusion.5), channel_id=1, source_target_pairs={{0,4},{4,0},{8,12},{12,8},{16,20},{20,16},{24,28},{28,24},{1,5},{5... | collective-permute-start | bytes 1179656 | tf_op jit(solution)/shard_map/ppermute | solution.py:598
  141.1 5.2 %collective-permute-start.12 = (bf16[2,128,768]{2,1,0:T(8,128)(2,1)S(1)}, bf16[2,128,768]{2,1,0:T(8,128)(2,1)S(1)}, u32[]{:S(2)}, u32[]{:S(2)}) collective-permute-start(bf16[2,128,768]{2,1,0:T(8,128)(2,1)S(1)} %dynamic-slice_bitcast_fusion.2), channel_id=1, source_target_pairs={{0,1},{1,0},{2,3},{3,2},{4,5},{5,4},{6,7},{7,6},{8,9},{9,8},{10,11... | collective-permute-start | bytes 1179656 | tf_op jit(solution)/shard_map/ppermute | solution.py:598
  146.7 14.8 %attend_backward_1.1 = (bf16[384,2048]{1,0:T(8,128)(2,1)}, bf16[512,384]{1,0:T(8,128)(2,1)}) custom-call(s32[8]{0:T(128)} %get-tuple-element.172.meta, bf16[512,2048]{1,0:T(8,128)(2,1)} %get-tuple-element.133.refs_0_, bf16[512,2048]{1,0:T(8,128)(2,1)} %get-tuple-element.143.refs_1_, bf16[512,2048]{1,0:T(8,128)(2,1)} %get-tuple-element.144.refs_2_, ...), custom_call_target="tpu_custom_call" | custom-call | flops 12000000000 | bytes 10000000 | tf_op jit(solution)/shard_map/attend_backward_1/pallas_call | solution.py:404
  161.8 5.0 %collective-permute-start.15 = (bf16[1,128,768]{2,1,0:T(8,128)(2,1)S(1)}, bf16[1,128,768]{2,1,0:T(8,128)(2,1)S(1)}, u32[]{:S(2)}, u32[]{:S(2)}) collective-permute-start(bf16[1,128,768]{2,1,0:T(8,128)(2,1)S(1)} %constant_dynamic-slice_fusion.2), channel_id=1, source_target_pairs={{0,2},{1,3},{2,0},{3,1},{4,6},{5,7},{6,4},{7,5},{8,10},{9,11},{10,... | collective-permute-start | bytes 589832 | tf_op jit(solution)/shard_map/ppermute | solution.py:598
  166.8 1.9 collective-permute-start.14
  168.8 14.6 %attend_backward_0.1 = (bf16[384,2048]{1,0:T(8,128)(2,1)}, bf16[512,384]{1,0:T(8,128)(2,1)}) custom-call(s32[8]{0:T(128)} %get-tuple-element.172.meta, bf16[512,2048]{1,0:T(8,128)(2,1)} %get-tuple-element.133.refs_0_, bf16[512,2048]{1,0:T(8,128)(2,1)} %get-tuple-element.143.refs_1_, bf16[512,2048]{1,0:T(8,128)(2,1)} %get-tuple-element.144.refs_2_, ...), custom_call_target="tpu_custom_call" | custom-call | flops 12000000000 | bytes 10000000 | tf_op jit(solution)/shard_map/attend_backward_0/pallas_call | solution.py:404
  184.6 3.1 %collective-permute-start.16 = (bf16[2,128,768]{2,1,0:T(8,128)(2,1)S(1)}, bf16[2,128,768]{2,1,0:T(8,128)(2,1)S(1)}, u32[]{:S(2)}, u32[]{:S(2)}) collective-permute-start(bf16[2,128,768]{2,1,0:T(8,128)(2,1)S(1)} %dynamic-slice_bitcast_fusion.1), channel_id=1, source_target_pairs={{0,1},{1,0},{2,3},{3,2},{4,5},{5,4},{6,7},{7,6},{8,9},{9,8},{10,11... | collective-permute-start | bytes 1179656 | tf_op jit(solution)/shard_map/ppermute | solution.py:598
  189.3 10.5 %input_side.1 = bf16[2048,512]{1,0:T(8,128)(2,1)} custom-call(s32[1]{0:T(128)} %bitcast.mine, bf16[128,1536]{1,0:T(8,128)(2,1)} %copy-done.3, bf16[128,1536]{1,0:T(8,128)(2,1)} %copy-done.7, bf16[128,1536]{1,0:T(8,128)(2,1)} %copy-done.6, bf16[128,1536]{1,0:T(8,128)(2,1)} %copy-done.8, bf16[384,2048]{1,0:T(8,128)(2,1)} %get-tuple-element.186.refs_4_, ...), custom_call_target="tpu_custom_call" | custom-call | flops 3300000000 | bytes 14000000 | tf_op jit(solution)/shard_map/input_side/pallas_call | solution.py:578
  199.9 24.2 %all_to_all.15 = bf16[8,16,1536]{2,1,0:T(8,128)(2,1)S(1)} all-to-all(bf16[8,16,1536]{2,1,0:T(8,128)(2,1)S(1)} %pad_maximum_fusion.3), channel_id=1, replica_groups=mesh['dp'=8,'fsdp'=4] {'dp'}, dimensions={0} | all-to-all | bytes 786432 | tf_op jit(solution)/shard_map/all_to_all | solution.py:690
  224.8 3.5 %all-to-all-start.1 = ((bf16[8,16,1536]{2,1,0:T(8,128)(2,1)}), bf16[8,16,1536]{2,1,0:T(8,128)(2,1)S(1)}, u32[]{:S(2)}, u32[]{:S(2)}) async-start(bf16[8,16,1536]{2,1,0:T(8,128)(2,1)} %tile.2), calls=%async_computation.1 | async-start | bytes 786432 | tf_op jit(solution)/shard_map/all_to_all | solution.py:692
  228.3 2.8 %collective-permute-start.18 = (bf16[128,1536]{1,0:T(8,128)(2,1)S(1)}, bf16[128,1536]{1,0:T(8,128)(2,1)S(1)}, u32[]{:S(2)}, u32[]{:S(2)}) collective-permute-start(bf16[128,1536]{1,0:T(8,128)(2,1)S(1)} %add_convert_fusion.1), channel_id=1, source_target_pairs={{0,16},{4,20},{8,24},{12,28},{16,0},{20,4},{24,8},{28,12},{1,17},{... | collective-permute-start | bytes 1179656 | tf_op jit(solution)/shard_map/ppermute | solution.py:598
  231.3 28.0 %collective-permute-done.19 = f32[32,512]{1,0:T(8,128)S(1)} collective-permute-done((f32[32,512]{1,0:T(8,128)S(1)}, f32[32,512]{1,0:T(8,128)S(1)}, u32[]{:S(2)}, u32[]{:S(2)}) %collective-permute-start.19) | collective-permute-done | bytes 65568 | tf_op jit(solution)/shard_map/ppermute | solution.py:598
  260.9 3.2 %moments.3 = (f32[128,512]{1,0:T(8,128)}, f32[128,512]{1,0:T(8,128)}, f32[128,512]{1,0:T(8,128)}, f32[128,512]{1,0:T(8,128)}, f32[128,512]{1,0:T(8,128)}, /*index=5*/f32[128,512]{1,0:T(8,128)}, f32[8,128]{1,0:T(8,128)}) custom-call(bf16[128,1536]{1,0:T(8,128)(2,1)} %add_convert_fusion.gradient, f32[128,512]{1,0:T(8,128)} %refs_3_.3, f32[128,512]{1,0:T(8,128)} %refs_1_.3, ...), custom_call_target="tpu_custom_call" | custom-call | flops 5000000 | bytes 5000000 | tf_op jit(solution)/shard_map/moments/pallas_call | solution.py:741
  264.9 3.4 %moments.2 = (f32[128,1536]{1,0:T(8,128)}, f32[128,1536]{1,0:T(8,128)}, f32[8,128]{1,0:T(8,128)}) custom-call(bf16[128,1536]{1,0:T(8,128)(2,1)} %bitcast.49, f32[128,1536]{1,0:T(8,128)} %refs_0_.5, f32[128,1536]{1,0:T(8,128)} %refs_1_.2, f32[128,1536]{1,0:T(8,128)} %refs_2_.2), custom_call_target="tpu_custom_call" | custom-call | flops 5000000 | bytes 5000000 | tf_op jit(solution)/shard_map/moments/pallas_call | solution.py:741
  269.1 5.6 %all-gather = f32[32,128]{1,0:T(8,128)} all-gather(f32[8,128]{1,0:T(8,128)S(1)} %pad_maximum_fusion.5), channel_id=2, replica_groups=mesh['dp'=8,'fsdp'=4] {'fsdp'}, dimensions={0}, use_global_device_ids=true | all-gather | bytes 20480 | tf_op jit(solution)/shard_map/all_gather | solution.py:884
  275.3 5.4 %apply.1 = (f32[128,1536]{1,0:T(8,128)}, bf16[128,1536]{1,0:T(8,128)(2,1)}, f32[128,512]{1,0:T(8,128)}, bf16[128,512]{1,0:T(8,128)(2,1)}, f32[128,512]{1,0:T(8,1...) custom-call(f32[4,8,128]{2,1,0:T(8,128)} %bitcast.53, ...), custom_call_target="tpu_custom_call" | custom-call | flops 5000000 | bytes 8000000 | tf_op jit(solution)/shard_map/apply/pallas_call | solution.py:776
  (117 shorter events, 21.3 us)
Async XLA Ops:
  1.9 12.8 %collective-permute-start.1 = (bf16[128,1536]{1,0:T(8,128)(2,1)S(1)}, bf16[128,1536]{1,0:T(8,128)(2,1)S(1)}, u32[]{:S(2)}, u32[]{:S(2)}) collective-permute-start(bf16[128,1536]{1,0:T(8,128)(2,1)S(1)} %convert_element_type.119.refs_0_), channel_id=1, source_target_pairs={{0,2},{1,3},{2,0},{3,1},{4,6},{5,7},{6,4},{7,5},{8,10},{9,11},{10,... | collective-permute-start | bytes 1179656 | tf_op jit(solution)/shard_map/ppermute | solution.py:598
  4.9 11.3 %collective-permute-start = (bf16[128,1536]{1,0:T(8,128)(2,1)S(1)}, bf16[128,1536]{1,0:T(8,128)(2,1)S(1)}, u32[]{:S(2)}, u32[]{:S(2)}) collective-permute-start(bf16[128,1536]{1,0:T(8,128)(2,1)S(1)} %convert_element_type.119.refs_0_), channel_id=1, source_target_pairs={{0,1},{1,0},{2,3},{3,2},{4,5},{5,4},{6,7},{7,6},{8,9},{9,8},{10,11... | collective-permute-start | bytes 1179656 | tf_op jit(solution)/shard_map/ppermute | solution.py:598
  14.6 2.6 collective-permute-start.2
  16.2 30.0 %copy-start.5 = (bf16[128,1664]{1,0:T(8,128)(2,1)}, bf16[128,1664]{1,0:T(8,128)(2,1)S(1)}, u32[]{:S(2)}) copy-start(bf16[128,1664]{1,0:T(8,128)(2,1)S(1)} %fusion.4.refs_0_) | copy-start | bytes 1277956
  17.3 29.0 %collective-permute-start.4 = (bf16[128,1664]{1,0:T(8,128)(2,1)S(1)}, bf16[128,1664]{1,0:T(8,128)(2,1)S(1)}, u32[]{:S(2)}, u32[]{:S(2)}) collective-permute-start(bf16[128,1664]{1,0:T(8,128)(2,1)S(1)} %fusion.4.refs_0_), channel_id=1, source_target_pairs={{0,2},{1,3},{2,0},{3,1},{4,6},{5,7},{6,4},{7,5},{8,10},{9,11},{10,... | collective-permute-start | bytes 1277960 | tf_op jit(solution)/shard_map/ppermute | solution.py:598
  17.5 36.1 %collective-permute-start.3 = (bf16[128,1664]{1,0:T(8,128)(2,1)S(1)}, bf16[128,1664]{1,0:T(8,128)(2,1)S(1)}, u32[]{:S(2)}, u32[]{:S(2)}) collective-permute-start(bf16[128,1664]{1,0:T(8,128)(2,1)S(1)} %fusion.4.refs_0_), channel_id=1, source_target_pairs={{0,1},{1,0},{2,3},{3,2},{4,5},{5,4},{6,7},{7,6},{8,9},{9,8},{10,11... | collective-permute-start | bytes 1277960 | tf_op jit(solution)/shard_map/ppermute | solution.py:598
  18.0 35.3 %copy-start.14 = (s32[1,4]{1,0:T(1,128)S(1)}, s32[1,4]{1,0:T(1,128)}, u32[]{:S(2)}) copy-start(s32[1,4]{1,0:T(1,128)} %param.26) | copy-start | bytes 52
  46.3 8.5 %collective-permute-start.5 = (bf16[128,1664]{1,0:T(8,128)(2,1)S(1)}, bf16[128,1664]{1,0:T(8,128)(2,1)S(1)}, u32[]{:S(2)}, u32[]{:S(2)}) collective-permute-start(bf16[128,1664]{1,0:T(8,128)(2,1)S(1)} %collective-permute-done.4.refs_2_), channel_id=1, source_target_pairs={{0,1},{1,0},{2,3},{3,2},{4,5},{5,4},{6,7},{7,6},{8,9},{9,8},{10,11... | collective-permute-start | bytes 1277960 | tf_op jit(solution)/shard_map/ppermute | solution.py:598
  85.3 15.1 %collective-permute-start.6 = (bf16[2,128,1536]{2,1,0:T(8,128)(2,1)S(1)}, bf16[2,128,1536]{2,1,0:T(8,128)(2,1)S(1)}, u32[]{:S(2)}, u32[]{:S(2)}) collective-permute-start(bf16[2,128,1536]{2,1,0:T(8,128)(2,1)S(1)} %dynamic-slice_bitcast_fusion), channel_id=1, source_target_pairs={{0,1},{1,0},{2,3},{3,2},{4,5},{5,4},{6,7},{7,6},{8,9},{9,8},{10,11... | collective-permute-start | bytes 2359304 | tf_op jit(solution)/shard_map/ppermute | solution.py:598
  85.6 14.7 %collective-permute-start.7 = (f32[32,512]{1,0:T(8,128)S(1)}, f32[32,512]{1,0:T(8,128)S(1)}, u32[]{:S(2)}, u32[]{:S(2)}) collective-permute-start(f32[32,512]{1,0:T(8,128)S(1)} %pad_maximum_fusion.4), channel_id=1, source_target_pairs={{0,1},{1,0},{2,3},{3,2},{4,5},{5,4},{6,7},{7,6},{8,9},{9,8},{10,11... | collective-permute-start | bytes 196616 | tf_op jit(solution)/shard_map/ppermute | solution.py:598
  100.7 19.6 %collective-permute-start.8 = (bf16[1,128,1536]{2,1,0:T(8,128)(2,1)S(1)}, bf16[1,128,1536]{2,1,0:T(8,128)(2,1)S(1)}, u32[]{:S(2)}, u32[]{:S(2)}) collective-permute-start(bf16[1,128,1536]{2,1,0:T(8,128)(2,1)S(1)} %constant_dynamic-slice_fusion.3), channel_id=1, source_target_pairs={{0,2},{1,3},{2,0},{3,1},{4,6},{5,7},{6,4},{7,5},{8,10},{9,11},{10,... | collective-permute-start | bytes 1179656 | tf_op jit(solution)/shard_map/ppermute | solution.py:598
  105.5 14.7 %collective-permute-start.9 = (f32[32,512]{1,0:T(8,128)S(1)}, f32[32,512]{1,0:T(8,128)S(1)}, u32[]{:S(2)}, u32[]{:S(2)}) collective-permute-start(f32[32,512]{1,0:T(8,128)S(1)} %fusion.12), channel_id=1, source_target_pairs={{0,2},{1,3},{2,0},{3,1},{4,6},{5,7},{6,4},{7,5},{8,10},{9,11},{10,... | collective-permute-start | bytes 196616 | tf_op jit(solution)/shard_map/ppermute | solution.py:598
  121.5 40.0 %collective-permute-start.10 = (bf16[128,1536]{1,0:T(8,128)(2,1)S(1)}, bf16[128,1536]{1,0:T(8,128)(2,1)S(1)}, u32[]{:S(2)}, u32[]{:S(2)}) collective-permute-start(bf16[128,1536]{1,0:T(8,128)(2,1)S(1)} %fusion.5), channel_id=1, source_target_pairs={{0,4},{4,0},{8,12},{12,8},{16,20},{20,16},{24,28},{28,24},{1,5},{5... | collective-permute-start | bytes 1179656 | tf_op jit(solution)/shard_map/ppermute | solution.py:598
  141.1 20.4 %collective-permute-start.12 = (bf16[2,128,768]{2,1,0:T(8,128)(2,1)S(1)}, bf16[2,128,768]{2,1,0:T(8,128)(2,1)S(1)}, u32[]{:S(2)}, u32[]{:S(2)}) collective-permute-start(bf16[2,128,768]{2,1,0:T(8,128)(2,1)S(1)} %dynamic-slice_bitcast_fusion.2), channel_id=1, source_target_pairs={{0,1},{1,0},{2,3},{3,2},{4,5},{5,4},{6,7},{7,6},{8,9},{9,8},{10,11... | collective-permute-start | bytes 1179656 | tf_op jit(solution)/shard_map/ppermute | solution.py:598
  146.3 15.2 %collective-permute-start.11 = (f32[32,512]{1,0:T(8,128)S(1)}, f32[32,512]{1,0:T(8,128)S(1)}, u32[]{:S(2)}, u32[]{:S(2)}) collective-permute-start(f32[32,512]{1,0:T(8,128)S(1)} %add.92), channel_id=1, source_target_pairs={{0,4},{4,0},{8,12},{12,8},{16,20},{20,16},{24,28},{28,24},{1,5},{5... | collective-permute-start | bytes 196616 | tf_op jit(solution)/shard_map/ppermute | solution.py:598
  161.8 21.6 %copy-start.9 = (bf16[512,384]{1,0:T(8,128)(2,1)S(1)}, bf16[512,384]{1,0:T(8,128)(2,1)}, u32[]{:S(2)}) copy-start(bf16[512,384]{1,0:T(8,128)(2,1)} %get-tuple-element.179) | copy-start | bytes 1179652
  161.8 21.6 %collective-permute-start.13 = (bf16[128,1536]{1,0:T(8,128)(2,1)S(1)}, bf16[128,1536]{1,0:T(8,128)(2,1)S(1)}, u32[]{:S(2)}, u32[]{:S(2)}) collective-permute-start(bf16[128,1536]{1,0:T(8,128)(2,1)S(1)} %add_convert_fusion.2), channel_id=1, source_target_pairs={{0,8},{4,12},{8,0},{12,4},{16,24},{20,28},{24,16},{28,20},{1,9},{5... | collective-permute-start | bytes 1179656 | tf_op jit(solution)/shard_map/ppermute | solution.py:598
  161.8 21.5 %collective-permute-start.15 = (bf16[1,128,768]{2,1,0:T(8,128)(2,1)S(1)}, bf16[1,128,768]{2,1,0:T(8,128)(2,1)S(1)}, u32[]{:S(2)}, u32[]{:S(2)}) collective-permute-start(bf16[1,128,768]{2,1,0:T(8,128)(2,1)S(1)} %constant_dynamic-slice_fusion.2), channel_id=1, source_target_pairs={{0,2},{1,3},{2,0},{3,1},{4,6},{5,7},{6,4},{7,5},{8,10},{9,11},{10,... | collective-permute-start | bytes 589832 | tf_op jit(solution)/shard_map/ppermute | solution.py:598
  166.8 16.5 %collective-permute-start.14 = (f32[32,512]{1,0:T(8,128)S(1)}, f32[32,512]{1,0:T(8,128)S(1)}, u32[]{:S(2)}, u32[]{:S(2)}) collective-permute-start(f32[32,512]{1,0:T(8,128)S(1)} %add.94), channel_id=1, source_target_pairs={{0,8},{4,12},{8,0},{12,4},{16,24},{20,28},{24,16},{28,20},{1,9},{5... | collective-permute-start | bytes 196616 | tf_op jit(solution)/shard_map/ppermute | solution.py:598
  184.6 4.4 %collective-permute-start.16 = (bf16[2,128,768]{2,1,0:T(8,128)(2,1)S(1)}, bf16[2,128,768]{2,1,0:T(8,128)(2,1)S(1)}, u32[]{:S(2)}, u32[]{:S(2)}) collective-permute-start(bf16[2,128,768]{2,1,0:T(8,128)(2,1)S(1)} %dynamic-slice_bitcast_fusion.1), channel_id=1, source_target_pairs={{0,1},{1,0},{2,3},{3,2},{4,5},{5,4},{6,7},{7,6},{8,9},{9,8},{10,11... | collective-permute-start | bytes 1179656 | tf_op jit(solution)/shard_map/ppermute | solution.py:598
  189.2 10.6 %collective-permute-start.17 = (bf16[1,128,768]{2,1,0:T(8,128)(2,1)S(1)}, bf16[1,128,768]{2,1,0:T(8,128)(2,1)S(1)}, u32[]{:S(2)}, u32[]{:S(2)}) collective-permute-start(bf16[1,128,768]{2,1,0:T(8,128)(2,1)S(1)} %constant_dynamic-slice_fusion.1), channel_id=1, source_target_pairs={{0,2},{1,3},{2,0},{3,1},{4,6},{5,7},{6,4},{7,5},{8,10},{9,11},{10,... | collective-permute-start | bytes 589832 | tf_op jit(solution)/shard_map/ppermute | solution.py:598
  224.8 34.5 %all-to-all-start.1 = ((bf16[8,16,1536]{2,1,0:T(8,128)(2,1)}), bf16[8,16,1536]{2,1,0:T(8,128)(2,1)S(1)}, u32[]{:S(2)}, u32[]{:S(2)}) async-start(bf16[8,16,1536]{2,1,0:T(8,128)(2,1)} %tile.2), calls=%async_computation.1 | async-start | bytes 786432 | tf_op jit(solution)/shard_map/all_to_all | solution.py:692
  228.3 31.0 %collective-permute-start.18 = (bf16[128,1536]{1,0:T(8,128)(2,1)S(1)}, bf16[128,1536]{1,0:T(8,128)(2,1)S(1)}, u32[]{:S(2)}, u32[]{:S(2)}) collective-permute-start(bf16[128,1536]{1,0:T(8,128)(2,1)S(1)} %add_convert_fusion.1), channel_id=1, source_target_pairs={{0,16},{4,20},{8,24},{12,28},{16,0},{20,4},{24,8},{28,12},{1,17},{... | collective-permute-start | bytes 1179656 | tf_op jit(solution)/shard_map/ppermute | solution.py:598
  231.1 28.2 %collective-permute-start.19 = (f32[32,512]{1,0:T(8,128)S(1)}, f32[32,512]{1,0:T(8,128)S(1)}, u32[]{:S(2)}, u32[]{:S(2)}) collective-permute-start(f32[32,512]{1,0:T(8,128)S(1)} %add.97), channel_id=1, source_target_pairs={{0,16},{4,20},{8,24},{12,28},{16,0},{20,4},{24,8},{28,12},{1,17},{... | collective-permute-start | bytes 196616 | tf_op jit(solution)/shard_map/ppermute | solution.py:598
  (15 other events, 122.0 us)
where the time goes:
time: 285 us; the launch traced here: 281 us
  Pallas kernels  144 us (51%)
  starting transfers between devices  59 us (21%)
  waiting for transfers between devices  31.6 us (11%)
  blocking collectives  29.8 us (10%)
  other arithmetic  9.9 us (3%)
  local copies, waits for them, and re-layouts  4.96 us (2%)
    pallas_call x4, Pallas kernels, backward(): pl.pallas_call(partial(backward_kernel, pair), grid=(1,), in_specs=[SMEM]...  58.5 us
    ppermute x20, starting transfers between devices, swap(): lax.ppermute(value, axis, [(index, index ^ mask) for index in range(size)])  55.6 us
    ppermute x20, waiting for transfers between devices, swap(): lax.ppermute(value, axis, [(index, index ^ mask) for index in range(size)])  31.6 us
    pallas_call x1, Pallas kernels, forward(): pl.pallas_call(partial(forward_kernel, count), grid=(PAIRS,), in_specs=[S...  28.2 us
    pallas_call x1, Pallas kernels, dense(): pl.pallas_call(partial(dense_kernel, count), grid=(length // block,), in_...  25.4 us
    all_to_all x1, blocking collectives, total_by_exchange(): lax.all_to_all(value, axis, 0, 0, tiled=True)  24.2 us
    pallas_call x1, Pallas kernels, input_side(): pl.pallas_call(partial(input_kernel, count), grid=(length // block,), in_...  10.5 us
    pallas_call x1, Pallas kernels, prep(): pl.pallas_call(prep_kernel, in_specs=[SMEM, SMEM, whole(1, length), whole...  9.01 us
  transfers between devices with their start and end apart: 21, of which 4 were waited for; matrix products, arithmetic and copies ran while one was open for 0% of the time, Pallas kernels for 38%

commit v1 on v0

--- a/solution.py
+++ b/solution.py
@@ -230,34 +230,38 @@
     pieces = refs[:count]
     tokens_t, packed, slot = refs[count : count + 3]
     q_out, k_out, v_out, kc_out, vc_out, kct_out, context, log_total = refs[count + 3 : count + 11]
-    weights, vct, side, total, shift, sem = refs[count + 11 :]
+    weights, kept_all, turned_all, vct, side, total, shift, sem = refs[count + 11 :]
     step = pl.program_id(0)
-    length = tokens_t.shape[1]
+    width, length = tokens_t.shape
 
     @pl.when(step == 0)
     def _():
-        fetch_rows(pieces, mine[0], weights, sem, 3)
-
-    columns = pl.ds(pl.multiple_of(step * 3 * PAIR, 3 * PAIR), 3 * PAIR)
-    part = weights[:, columns]
+        fetch_rows(pieces, mine[0], weights, sem)
+
+        def project(begin, rows, *_):
+            place = pl.ds(begin, rows)
+            both = mm(packed[place, :], weights[:, width:], NN)
+            kept_all[place, :] = both.astype(BF)
+            turned_all[:, place] = both.T.astype(BF)
+
+        walk(meta, length, project)
+
+    def here(kind):
+        return pl.ds(pl.multiple_of(kind * width + step * PAIR, PAIR), PAIR)
+
+    part = jnp.concatenate([weights[:, here(kind)] for kind in range(3)], axis=1)
     joined = mm(part, tokens_t[...], TN)
     q_out[...] = (joined[:PAIR] * HDIM**-0.5).astype(BF)
     k_out[...] = joined[PAIR : 2 * PAIR].astype(BF)
     v_out[...] = joined[2 * PAIR :].astype(BF)
-
-    def project(begin, rows, *_):
-        place = pl.ds(begin, rows)
-        both = mm(packed[place, :], part[:, PAIR:], NN).astype(BF)
-        kc_out[place, :] = both[:, :PAIR]
-        vc_out[place, :] = both[:, PAIR:]
-        kct_out[:, place] = both[:, :PAIR].T
-        turned = both[:, PAIR:].T
-        ones = jnp.where(iota((16, rows), 0) == 0, 1.0, 0.0).astype(BF)
-        for head in range(2):
-            vct[head, :HDIM, place] = turned[HDIM * head : HDIM * (head + 1)]
-            vct[head, HDIM:, place] = ones
-
-    walk(meta, length, project)
+    kc_out[...] = kept_all[:, here(0)]
+    vc_out[...] = kept_all[:, here(1)]
+    kct_out[...] = turned_all[here(0), :]
+    ones = jnp.where(iota((16, length), 0) == 0, 1.0, 0.0).astype(BF)
+    for head in range(2):
+        begin = pl.multiple_of(width + step * PAIR + HDIM * head, HDIM)
+        vct[head, :HDIM, :] = turned_all[pl.ds(begin, HDIM), :]
+        vct[head, HDIM:, :] = ones
 
     masked = slot[...] < 0
     own = []
@@ -303,7 +307,7 @@
         alone = jnp.exp(own[head] - shift[head : head + 1, :])
         row_total = total[head, HDIM : HDIM + 1, :] + alone
         gathered = total[head, :HDIM, :] + v_out[rows, :].astype(F32) * alone
-        context[rows, :] = (gathered / row_total).astype(BF)
+        context[rows, :] = (gathered * (1.0 / row_total)).astype(BF)
         log_total[pl.ds(step * 2 + head, 1), :] = shift[head : head + 1, :] + jnp.log(row_total)
 
 
@@ -327,11 +331,13 @@
         + [jax.ShapeDtypeStruct((HEADS, length), F32)],
         scratch_shapes=[
             pltpu.VMEM((width, 3 * width), BF),
+            pltpu.VMEM((length, 2 * width), BF),
+            pltpu.VMEM((2 * width, length), BF),
             pltpu.VMEM((2, HDIM + 16, length), BF),
             pltpu.VMEM((2, PAIR, length), BF),
             pltpu.VMEM((2, HDIM + 16, length), F32),
             pltpu.VMEM((8, length), F32),
-            pltpu.SemaphoreType.DMA((3 * PAIRS * count,)),
+            pltpu.SemaphoreType.DMA((count,)),
         ],
         compiler_params=params(56),
         cost_estimate=cost(15e9, 25e6, 20e6),
@@ -454,8 +460,8 @@
 def dense_kernel(count, mine, *refs):
     pieces = refs[:count]
     tokens_t, context, cot_t = refs[count : count + 3]
-    out, grad_context, grad_first, inner, g_proj, g_up, g_down, g_norm = refs[count + 3 : count + 11]
-    weights, total, norm_total, sem = refs[count + 11 :]
+    out, grad_context, grad_first, inner, g_side, g_norm = refs[count + 3 : count + 9]
+    weights, total, norm_total, sem = refs[count + 9 :]
     step = pl.program_id(0)
     width = tokens_t.shape[0]
 
@@ -471,44 +477,58 @@
     rows = weights[:, 3 * width :].astype(F32)
     gain1, bias1, gain2, bias2 = (rows[:, index : index + 1] for index in range(4))
 
-    context_low = context[...]
-    scaled1, scale1 = normalise(tokens_t[...].astype(F32) + mm(proj, context_low, TN))
-    middle = scaled1 * gain1 + bias1
-    middle_low = middle.astype(BF)
-    hidden = mm(up, middle_low, TN)
-    cdf = 0.5 * (1.0 + lax.erf(hidden * 2.0**-0.5))
-    slope = cdf + hidden * jnp.exp(hidden * hidden * -0.5) * 0.3989422804014327
-    active = (hidden * cdf).astype(BF)
-    scaled2, scale2 = normalise(middle + mm(down, active, TN))
-    out[...] = (scaled2 * gain2 + bias2).astype(BF).T
-
-    cot = cot_t[...].astype(F32)
-    norm_total[2] += lane_sums(cot * scaled2)
-    norm_total[3] += lane_sums(cot)
-    grad_second = pull_norm(cot, scaled2, scale2, gain2)
-    grad_low = grad_second.astype(BF)
-    total[2] += mm(active, grad_low, NT)
-    grad_hidden = (mm(down, grad_low, NN) * slope).astype(BF)
-    total[1] += mm(middle_low, grad_hidden, NT)
-    grad_middle = grad_second + mm(up, grad_hidden, NN)
-    norm_total[0] += lane_sums(grad_middle * scaled1)
-    norm_total[1] += lane_sums(grad_middle)
-    grad_h1 = pull_norm(grad_middle, scaled1, scale1, gain1)
-    grad_first[...] = grad_h1
-    proj_low = grad_h1.astype(BF)
-    total[0] += mm(context_low, proj_low, NT)
-    pulled = mm(proj, proj_low, NN).astype(BF)
-    grad_context[...] = pulled
-    both = pulled.astype(F32) * context_low.astype(F32)
-    for head in range(HEADS):
-        part = both[HDIM * head : HDIM * (head + 1), :]
-        inner[head : head + 1, :] = jnp.sum(part, axis=0, keepdims=True)
+    def half(place):
+        context_low = context[:, place]
+        first_sum = tokens_t[:, place].astype(F32) + mm(proj, context_low, TN)
+        yield
+        scaled1, scale1 = normalise(first_sum)
+        middle = scaled1 * gain1 + bias1
+        middle_low = middle.astype(BF)
+        hidden = mm(up, middle_low, TN)
+        yield
+        cdf = 0.5 * (1.0 + lax.erf(hidden * 2.0**-0.5))
+        slope = cdf + hidden * jnp.exp(hidden * hidden * -0.5) * 0.3989422804014327
+        active = (hidden * cdf).astype(BF)
+        second_sum = middle + mm(down, active, TN)
+        yield
+        scaled2, scale2 = normalise(second_sum)
+        out[place, :] = (scaled2 * gain2 + bias2).astype(BF).T
+        cot = cot_t[:, place].astype(F32)
+        norm_total[2] += lane_sums(cot * scaled2)
+        norm_total[3] += lane_sums(cot)
+        grad_second = pull_norm(cot, scaled2, scale2, gain2)
+        grad_low = grad_second.astype(BF)
+        pulled = mm(down, grad_low, NN)
+        total[2] += mm(active, grad_low, NT)
+        yield
+        grad_hidden = (pulled * slope).astype(BF)
+        grad_middle = grad_second + mm(up, grad_hidden, NN)
+        total[1] += mm(middle_low, grad_hidden, NT)
+        yield
+        norm_total[0] += lane_sums(grad_middle * scaled1)
+        norm_total[1] += lane_sums(grad_middle)
+        grad_h1 = pull_norm(grad_middle, scaled1, scale1, gain1)
+        grad_first[:, place] = grad_h1
+        proj_low = grad_h1.astype(BF)
+        pulled = mm(proj, proj_low, NN)
+        total[0] += mm(context_low, proj_low, NT)
+        yield
+        pulled = pulled.astype(BF)
+        grad_context[:, place] = pulled
+        both = pulled.astype(F32) * context_low.astype(F32)
+        for head in range(HEADS):
+            part = both[HDIM * head : HDIM * (head + 1), :]
+            inner[head : head + 1, place] = jnp.sum(part, axis=0, keepdims=True)
+
+    columns = tokens_t.shape[1] // 2
+    halves = [half(slice(columns * index, columns * (index + 1))) for index in range(2)]
+    while halves:
+        halves = [stage for stage in halves if next(stage, stage) is None]
 
     @pl.when(step == pl.num_programs(0) - 1)
     def _():
-        g_proj[...] = total[0].astype(BF)
-        g_up[...] = total[1].astype(BF)
-        g_down[...] = total[2].astype(BF)
+        for index in range(3):
+            g_side[:, width * index : width * (index + 1)] = total[index].astype(BF)
         lane = iota((width, 128), 1)
         packed = jnp.zeros((width, 128), F32)
         for index in range(4):
@@ -519,10 +539,9 @@
 
 def dense(mine, pieces, tokens_t, context, cot_t):
     width, length = tokens_t.shape
-    block = 512
+    block = 1024
     count = len(pieces)
     columns = pl.BlockSpec((width, block), lambda step: (0, step))
-    square = jax.ShapeDtypeStruct((width, width), BF)
     return pl.pallas_call(
         partial(dense_kernel, count),
         grid=(length // block,),
@@ -533,16 +552,15 @@
             columns,
             pl.BlockSpec((HEADS, block), lambda step: (0, step)),
         ]
-        + [whole(width, width)] * 3
-        + [whole(width, 128)],
+        + [whole(width, 3 * width), whole(width, 128)],
         out_shape=[
             jax.ShapeDtypeStruct((length, width), BF),
             jax.ShapeDtypeStruct((width, length), BF),
             jax.ShapeDtypeStruct((width, length), F32),
             jax.ShapeDtypeStruct((HEADS, length), F32),
-        ]
-        + [square] * 3
-        + [jax.ShapeDtypeStruct((width, 128), F32)],
+            jax.ShapeDtypeStruct((width, 3 * width), BF),
+            jax.ShapeDtypeStruct((width, 128), F32),
+        ],
         scratch_shapes=[
             pltpu.VMEM((width, 3 * width + 128), BF),
             pltpu.VMEM((3, width, width), F32),
@@ -711,7 +729,11 @@
 def moments_kernel(count, paired, gradient, *refs):
     olds, outs, squares = refs[: 3 * count], refs[3 * count : 5 * count], refs[5 * count]
     at = 0
-    squares[...] = jnp.zeros(squares.shape, F32)
+
+    @pl.when(pl.program_id(0) == 0)
+    def _():
+        squares[...] = jnp.zeros(squares.shape, F32)
+
     for index in range(count):
         weight, first_old, second_old = (ref[...] for ref in olds[3 * index : 3 * index + 3])
         columns = weight.shape[1]
@@ -730,18 +752,29 @@
         outs[2 * index][...] = first_new
         outs[2 * index + 1][...] = second_new
         update = update_of(first_new, second_new) + MATRIX_DECAY * weight
-        squares[index : index + 1, :] = square_row(weight)
-        squares[4 + index : 5 + index, :] = square_row(update)
+        squares[index : index + 1, :] += square_row(weight)
+        squares[4 + index : 5 + index, :] += square_row(update)
+
+
+def row_blocks(arrays):
+    rows = arrays[0].shape[0]
+    steps = rows // 32 if rows % 32 == 0 else 1
+    return steps, [
+        pl.BlockSpec((rows // steps, array.shape[1]), lambda step: (step, 0)) for array in arrays
+    ]
 
 
 def new_moments(gradient, olds, paired):
-    shapes = [jax.ShapeDtypeStruct(old.shape, F32) for old in olds]
     count = len(olds) // 3
-    outs = [shape for shape in shapes[::3] for _ in range(2)]
+    outs = [jax.ShapeDtypeStruct(old.shape, F32) for old in olds[::3] for _ in range(2)]
+    steps, in_specs = row_blocks((gradient, *olds))
     results = pl.pallas_call(
         partial(moments_kernel, count, paired),
+        grid=(steps,),
+        in_specs=in_specs,
+        out_specs=row_blocks(outs)[1] + [whole(8, 128)],
         out_shape=outs + [jax.ShapeDtypeStruct((8, 128), F32)],
-        compiler_params=params(56),
+        compiler_params=params(32),
         cost_estimate=cost(5e6, 5e6),
         name="moments",
     )(gradient, *olds)
@@ -773,10 +806,14 @@
     outs = []
     for weight in arrays[::3]:
         outs += [jax.ShapeDtypeStruct(weight.shape, F32), jax.ShapeDtypeStruct(weight.shape, BF)]
+    steps, in_specs = row_blocks(arrays)
     results = pl.pallas_call(
         partial(apply_kernel, count),
+        grid=(steps,),
+        in_specs=[whole(*squares.shape)] + in_specs,
+        out_specs=row_blocks(outs)[1] + [whole(3, 4)],
         out_shape=outs + [jax.ShapeDtypeStruct((3, 4), F32)],
-        compiler_params=params(56),
+        compiler_params=params(32),
         cost_estimate=cost(5e6, 8e6),
         name="apply",
     )(squares, *arrays)
@@ -823,10 +860,12 @@
         mine_ref, meta, qkv_pieces, tokens_t, packed, slot
     )
     rest_pieces = gather_pieces(rest, "fsdp", fsdp, q_t)
-    out, grad_context, grad_first, inner, g_proj, g_up, g_down, g_norm = dense(
+    out, grad_context, grad_first, inner, g_side, g_norm = dense(
         mine_ref, rest_pieces, tokens_t, context, cot_t
     )
 
+    side_chain = Chain(side_steps(g_side, fsdp, dp))
+    g_norm = start_steps(g_norm, [side_chain])
     first_cells = out.reshape(-1, SHORT_LENGTH, width)[:, 0, :].astype(F32)
     slot_index = jnp.arange(first_cells.shape[0], dtype=jnp.int32)
     used_slots = (cell_kind[0] == 0) | (slot_index == 0)
@@ -838,8 +877,9 @@
     sums = jnp.sum(member[:, :, None] * first_cells[:, None, :], axis=0)
     squares = jnp.sum(member[:, :, None] * (first_cells * first_cells)[:, None, :], axis=0)
     small = jnp.concatenate([counts, sums, squares, g_norm[:, :8].T], axis=0)
+    small, meta = lax.optimization_barrier((small, meta))
     small_chain = Chain(small_steps(small, fsdp, dp))
-    side_chain = Chain(side_steps(jnp.concatenate([g_proj, g_up, g_down], axis=1), fsdp, dp))
+    meta = end_steps(meta, [side_chain])
     chains = [side_chain, small_chain]
     half_chains = []
     grads = []
@@ -856,15 +896,19 @@
             half_chains.append(Chain(halving(jnp.concatenate(parts, axis=1), "fsdp", fsdp)))
             chains.append(half_chains[-1])
             parts = []
-    mine_ref = start_steps(mine_ref, chains)
-    mine_ref = end_steps(mine_ref, half_chains)
-    mine_ref = start_steps(mine_ref, half_chains)
+    late = half_chains[-1:]
+    side_share = side_chain.finish()
+    side_share = start_steps(side_share, late)
+    side_old = (proj_weight, proj_first, proj_second, up_weight, up_first, up_second)
+    side_old += (down_weight, down_first, down_second)
+    side_new, side_squares = new_moments(side_share, side_old, False)
+    side_squares = end_steps(side_squares, late)
+    mine_ref, side_squares = lax.optimization_barrier((mine_ref, side_squares))
+    mine_ref = start_steps(mine_ref, late + [small_chain])
     input_grad = input_side(mine_ref, qkv_pieces, grads[::-1], grad_first)
-    input_grad = end_steps(input_grad, half_chains)
+    input_grad = end_steps(input_grad, late + [small_chain])
     qkv_share = jnp.concatenate([chain.finish() for chain in half_chains], axis=1)
     qkv_share = total_by_exchange(qkv_share, "dp", dp)
-    qkv_share = end_steps(qkv_share, chains)
-    side_share = side_chain.finish()
     small = small_chain.finish()
     study_mean = small[8:16] / small[:8]
     study_var = small[16:24] / small[:8] - study_mean * study_mean
@@ -872,12 +916,9 @@
     norm_first, norm_second = moments(norm_share, norm_first, norm_second)
     norm_params = norm_params - VECTOR_RATE * update_of(norm_first, norm_second)
 
-    side_old = (proj_weight, proj_first, proj_second, up_weight, up_first, up_second)
-    side_old += (down_weight, down_first, down_second)
     (qkv_first, qkv_second), qkv_squares = new_moments(
         qkv_share, (qkv_weight, qkv_first, qkv_second), True
     )
-    side_new, side_squares = new_moments(side_share, side_old, False)
     squares = jnp.concatenate(
         [qkv_squares[0:1], side_squares[0:3], qkv_squares[4:5], side_squares[4:7]], axis=0
     )

time: 285 us -> 265 us (0.930)
  Pallas kernels: 144 us -> 181 us
  starting transfers between devices: 59 us -> 26.9 us
  waiting for transfers between devices: 31.6 us -> 11.1 us
  blocking collectives: 29.8 us -> 20.1 us
  local copies, waits for them, and re-layouts: 4.96 us -> 9.2 us
    ppermute x20, starting transfers between devices: 55.6 us -> 23.4 us  [swap(): lax.ppermute(value, axis, [(index, index ^ mask) for index in range(size)])]
    ppermute x20, waiting for transfers between devices: 31.6 us -> 2.97 us  [swap(): lax.ppermute(value, axis, [(index, index ^ mask) for index in range(size)])]
    pallas_call x4, Pallas kernels: 58.5 us -> 84.1 us  [backward(): pl.pallas_call(partial(backward_kernel, pair), grid=(1,), in_specs=[SMEM]...]
    pallas_call x1, Pallas kernels: 28.2 us -> 47.1 us  [forward(): pl.pallas_call(partial(forward_kernel, count), grid=(PAIRS,), in_specs=[S...]
    all_to_all x1, blocking collectives: 24.2 us -> 14.9 us  [total_by_exchange(): lax.all_to_all(value, axis, 0, 0, tiled=True)]
    all_to_all x1, waiting for transfers between devices: 0.01 us -> 8.1 us  [total_by_exchange(): return lax.all_to_all(jnp.tile(mine, (size, 1)), axis, 0, 0, tiled=True)]
    pallas_call x3, Pallas kernels: 12 us -> 6.8 us  [the longest x2 3.99 us: new_moments(): pl.pallas_call(partial(moments_kernel, count, paired), grid=(steps,), in_...]
  transfers between devices with their start and end apart: 21 -> 21, of which waited for: 4 -> 3; matrix products, arithmetic and copies ran while one was open for 0% -> 2% of each run, Pallas kernels for 38% -> 59%
where the time goes in v1:
time: 265 us; the launch traced here: 261 us
  Pallas kernels  181 us (68%)
  starting transfers between devices  26.9 us (10%)
  blocking collectives  20.1 us (8%)
  waiting for transfers between devices  11.1 us (4%)
  other arithmetic  9.84 us (4%)
  local copies, waits for them, and re-layouts  9.2 us (3%)
    pallas_call x4, Pallas kernels, backward(): pl.pallas_call(partial(backward_kernel, pair), grid=(1,), in_specs=[SMEM]...  84.1 us
    pallas_call x1, Pallas kernels, forward(): pl.pallas_call(partial(forward_kernel, count), grid=(PAIRS,), in_specs=[S...  47.1 us
    ppermute x20, starting transfers between devices, swap(): lax.ppermute(value, axis, [(index, index ^ mask) for index in range(size)])  23.4 us
    pallas_call x1, Pallas kernels, dense(): pl.pallas_call(partial(dense_kernel, count), grid=(length // block,), in_...  23.1 us
    all_to_all x1, blocking collectives, total_by_exchange(): lax.all_to_all(value, axis, 0, 0, tiled=True)  14.9 us
    pallas_call x1, Pallas kernels, input_side(): pl.pallas_call(partial(input_kernel, count), grid=(length // block,), in_...  10.4 us
    pallas_call x1, Pallas kernels, prep(): pl.pallas_call(prep_kernel, in_specs=[SMEM, SMEM, whole(1, length), whole...  9.67 us
    all_to_all x1, waiting for transfers between devices, total_by_exchange(): return lax.all_to_all(jnp.tile(mine, (size, 1)), axis, 0, 0, tiled=True)  8.1 us
  transfers between devices with their start and end apart: 21, of which 3 were waited for; matrix products, arithmetic and copies ran while one was open for 2% of the time, Pallas kernels for 59%

profile of v1, /device:TPU:0, one launch (start us, length us, event | category | flops | bytes accessed | tf_op | source)
XLA Modules:
  0.0 260.7 jit_solution(3589139427074793513)
XLA Ops:
  1.9 3.0 %collective-permute-start.1 = (bf16[128,1536]{1,0:T(8,128)(2,1)S(1)}, bf16[128,1536]{1,0:T(8,128)(2,1)S(1)}, u32[]{:S(2)}, u32[]{:S(2)}) collective-permute-start(bf16[128,1536]{1,0:T(8,128)(2,1)S(1)} %convert_element_type.119.refs_0_), channel_id=1, source_target_pairs={{0,2},{1,3},{2,0},{3,1},{4,6},{5,7},{6,4},{7,5},{8,10},{9,11},{10,... | collective-permute-start | bytes 1179656 | tf_op jit(solution)/shard_map/ppermute | solution.py:616
  5.6 9.7 %prep.1 = (bf16[512,2048]{1,0:T(8,128)(2,1)}, bf16[512,2048]{1,0:T(8,128)(2,1)}, bf16[2048,512]{1,0:T(8,128)(2,1)}, s32[1,2048]{1,0:T(1,128)}, s32[8]{0:T(128)}) custom-call(s32[1]{0:T(128)S(6)} %copy.82.kind, s32[4]{0:T(128)} %bitcast.61, s32[1,2048]{1,0:T(1,128)} %known.1, bf16[2048,512]{1,0:T(8,128)(2,1)} %bitcast.59, bf16[2048,512]{1,0:T(8,128)(2,1)} %bitcast.60), custom_call_target="tpu_custom_call" | custom-call | flops 3000000000 | bytes 12000000 | tf_op jit(solution)/shard_map/prep/pallas_call | solution.py:115
  15.7 1.4 collective-permute-done.2.refs_3_
  17.8 47.1 %attend_forward.1 = (bf16[512,2048]{1,0:T(8,128)(2,1)}, bf16[512,2048]{1,0:T(8,128)(2,1)}, bf16[512,2048]{1,0:T(8,128)(2,1)}, bf16[2048,512]{1,0:T(8,128)(2,1)},...) custom-call(s32[1]{0:T(128)} %bitcast.mine, ...), custom_call_target="tpu_custom_call" | custom-call | flops 15000000512 | bytes 25000000 | tf_op jit(solution)/shard_map/attend_forward/pallas_call | solution.py:321
  65.3 1.6 collective-permute-done.5.refs_3_
  67.6 23.1 %dense.1 = (bf16[2048,512]{1,0:T(8,128)(2,1)}, bf16[512,2048]{1,0:T(8,128)(2,1)}, f32[512,2048]{1,0:T(8,128)}, f32[8,2048]{1,0:T(8,128)}, bf16[512,1536]{1,0:T(8,128)(2,1)}, /*index=5*/f32[512,128]{1,0:T(8,128)}) custom-call(s32[1]{0:T(128)} %bitcast.mine, bf16[128,1664]{1,0:T(8,128)(2,1)} %copy-done.22, bf16[128,1664]{1,0:T(8,128)(2,1)} %collective-permute-done.3.refs_1_, ...), custom_call_target="tpu_custom_call" | custom-call | flops 10000000000 | bytes 20000000 | tf_op jit(solution)/shard_map/dense/pallas_call | solution.py:545
  90.8 2.2 dynamic-slice_bitcast_fusion
  96.1 1.8 collective-permute-start.7
  97.9 18.9 %attend_backward_3.1 = (bf16[384,2048]{1,0:T(8,128)(2,1)}, bf16[512,384]{1,0:T(8,128)(2,1)}) custom-call(s32[8]{0:T(128)} %get-tuple-element.179.meta, bf16[512,2048]{1,0:T(8,128)(2,1)} %get-tuple-element.136.refs_0_, bf16[512,2048]{1,0:T(8,128)(2,1)} %get-tuple-element.150.refs_1_, bf16[512,2048]{1,0:T(8,128)(2,1)} %get-tuple-element.151.refs_2_, ...), custom_call_target="tpu_custom_call" | custom-call | flops 12000000000 | bytes 10000000 | tf_op jit(solution)/shard_map/attend_backward_3/pallas_call | solution.py:410
  117.5 27.3 %attend_backward_2.1 = (bf16[384,2048]{1,0:T(8,128)(2,1)}, bf16[512,384]{1,0:T(8,128)(2,1)}) custom-call(s32[8]{0:T(128)} %get-tuple-element.179.meta, bf16[512,2048]{1,0:T(8,128)(2,1)} %get-tuple-element.136.refs_0_, bf16[512,2048]{1,0:T(8,128)(2,1)} %get-tuple-element.150.refs_1_, bf16[512,2048]{1,0:T(8,128)(2,1)} %get-tuple-element.151.refs_2_, ...), custom_call_target="tpu_custom_call" | custom-call | flops 12000000000 | bytes 10000000 | tf_op jit(solution)/shard_map/attend_backward_2/pallas_call | solution.py:410
  146.2 1.8 collective-permute-start.12
  148.1 18.9 %attend_backward_1.1 = (bf16[384,2048]{1,0:T(8,128)(2,1)}, bf16[512,384]{1,0:T(8,128)(2,1)}) custom-call(s32[8]{0:T(128)} %get-tuple-element.179.meta, bf16[512,2048]{1,0:T(8,128)(2,1)} %get-tuple-element.136.refs_0_, bf16[512,2048]{1,0:T(8,128)(2,1)} %get-tuple-element.150.refs_1_, bf16[512,2048]{1,0:T(8,128)(2,1)} %get-tuple-element.151.refs_2_, ...), custom_call_target="tpu_custom_call" | custom-call | flops 12000000000 | bytes 10000000 | tf_op jit(solution)/shard_map/attend_backward_1/pallas_call | solution.py:410
  167.3 7.4 %collective-permute-start.14 = (bf16[128,1536]{1,0:T(8,128)(2,1)S(1)}, bf16[128,1536]{1,0:T(8,128)(2,1)S(1)}, u32[]{:S(2)}, u32[]{:S(2)}) collective-permute-start(bf16[128,1536]{1,0:T(8,128)(2,1)S(1)} %add_convert_fusion.1), channel_id=1, source_target_pairs={{0,16},{4,20},{8,24},{12,28},{16,0},{20,4},{24,8},{28,12},{1,17},{... | collective-permute-start | bytes 1179656 | tf_op jit(solution)/shard_map/ppermute | solution.py:616
  176.4 19.0 %attend_backward_0.1 = (bf16[384,2048]{1,0:T(8,128)(2,1)}, bf16[512,384]{1,0:T(8,128)(2,1)}) custom-call(s32[8]{0:T(128)} %get-tuple-element.179.meta, bf16[512,2048]{1,0:T(8,128)(2,1)} %get-tuple-element.136.refs_0_, bf16[512,2048]{1,0:T(8,128)(2,1)} %get-tuple-element.150.refs_1_, bf16[512,2048]{1,0:T(8,128)(2,1)} %get-tuple-element.151.refs_2_, ...), custom_call_target="tpu_custom_call" | custom-call | flops 12000000000 | bytes 10000000 | tf_op jit(solution)/shard_map/attend_backward_0/pallas_call | solution.py:410
  196.9 2.0 moments.2
  199.1 5.3 %collective-permute-start.18 = (bf16[1,128,768]{2,1,0:T(8,128)(2,1)S(1)}, bf16[1,128,768]{2,1,0:T(8,128)(2,1)S(1)}, u32[]{:S(2)}, u32[]{:S(2)}) collective-permute-start(bf16[1,128,768]{2,1,0:T(8,128)(2,1)S(1)} %constant_dynamic-slice_fusion.1), channel_id=1, source_target_pairs={{0,2},{1,3},{2,0},{3,1},{4,6},{5,7},{6,4},{7,5},{8,10},{9,11},{10,... | collective-permute-start | bytes 589832 | tf_op jit(solution)/shard_map/ppermute | solution.py:616
  205.4 10.4 %input_side.1 = bf16[2048,512]{1,0:T(8,128)(2,1)} custom-call(s32[1]{0:T(128)} %bitcast.mine, bf16[128,1536]{1,0:T(8,128)(2,1)} %copy-done.20, bf16[128,1536]{1,0:T(8,128)(2,1)} %copy-done.24, bf16[128,1536]{1,0:T(8,128)(2,1)} %copy-done.23, bf16[128,1536]{1,0:T(8,128)(2,1)} %copy-done.25, bf16[384,2048]{1,0:T(8,128)(2,1)} %get-tuple-element.195.refs_4_, ...), custom_call_target="tpu_custom_call" | custom-call | flops 3300000000 | bytes 14000000 | tf_op jit(solution)/shard_map/input_side/pallas_call | solution.py:596
  216.5 14.9 %all_to_all.14 = bf16[8,16,1536]{2,1,0:T(8,128)(2,1)S(1)} all-to-all(bf16[8,16,1536]{2,1,0:T(8,128)(2,1)S(1)} %pad_maximum_fusion.2), channel_id=1, replica_groups=mesh['dp'=8,'fsdp'=4] {'dp'}, dimensions={0} | all-to-all | bytes 786432 | tf_op jit(solution)/shard_map/all_to_all | solution.py:708
  232.1 1.6 tile.2
  233.7 3.5 %all-to-all-start.1 = ((bf16[8,16,1536]{2,1,0:T(8,128)(2,1)}), bf16[8,16,1536]{2,1,0:T(8,128)(2,1)S(1)}, u32[]{:S(2)}, u32[]{:S(2)}) async-start(bf16[8,16,1536]{2,1,0:T(8,128)(2,1)} %tile.2), calls=%async_computation.1 | async-start | bytes 786432 | tf_op jit(solution)/shard_map/all_to_all | solution.py:710
  240.0 8.1 %all-to-all-done.1 = bf16[8,16,1536]{2,1,0:T(8,128)(2,1)S(1)} async-done(((bf16[8,16,1536]{2,1,0:T(8,128)(2,1)}), bf16[8,16,1536]{2,1,0:T(8,128)(2,1)S(1)}, u32[]{:S(2)}, u32[]{:S(2)}) %all-to-all-start.1) | async-done | bytes 393248 | tf_op jit(solution)/shard_map/all_to_all | solution.py:710
  248.2 2.0 moments.3
  250.2 5.2 %all-gather = f32[32,128]{1,0:T(8,128)S(1)} all-gather(f32[8,128]{1,0:T(8,128)S(1)} %pad_maximum_fusion.4), channel_id=2, replica_groups=mesh['dp'=8,'fsdp'=4] {'fsdp'}, dimensions={0}, use_global_device_ids=true | all-gather | bytes 20480 | tf_op jit(solution)/shard_map/all_gather | solution.py:925
  257.7 2.8 %apply.1 = (f32[128,1536]{1,0:T(8,128)}, bf16[128,1536]{1,0:T(8,128)(2,1)}, f32[128,512]{1,0:T(8,128)}, bf16[128,512]{1,0:T(8,128)(2,1)}, f32[128,512]{1,0:T(8,1...) custom-call(f32[4,8,128]{2,1,0:T(8,128)S(1)} %bitcast.43, ...), custom_call_target="tpu_custom_call" | custom-call | flops 5000000 | bytes 8000000 | tf_op jit(solution)/shard_map/apply/pallas_call | solution.py:810
  (148 shorter events, 19.4 us)
Async XLA Ops:
  1.9 13.4 %collective-permute-start.1 = (bf16[128,1536]{1,0:T(8,128)(2,1)S(1)}, bf16[128,1536]{1,0:T(8,128)(2,1)S(1)}, u32[]{:S(2)}, u32[]{:S(2)}) collective-permute-start(bf16[128,1536]{1,0:T(8,128)(2,1)S(1)} %convert_element_type.119.refs_0_), channel_id=1, source_target_pairs={{0,2},{1,3},{2,0},{3,1},{4,6},{5,7},{6,4},{7,5},{8,10},{9,11},{10,... | collective-permute-start | bytes 1179656 | tf_op jit(solution)/shard_map/ppermute | solution.py:616
  4.9 10.8 %collective-permute-start = (bf16[128,1536]{1,0:T(8,128)(2,1)S(1)}, bf16[128,1536]{1,0:T(8,128)(2,1)S(1)}, u32[]{:S(2)}, u32[]{:S(2)}) collective-permute-start(bf16[128,1536]{1,0:T(8,128)(2,1)S(1)} %convert_element_type.119.refs_0_), channel_id=1, source_target_pairs={{0,1},{1,0},{2,3},{3,2},{4,5},{5,4},{6,7},{7,6},{8,9},{9,8},{10,11... | collective-permute-start | bytes 1179656 | tf_op jit(solution)/shard_map/ppermute | solution.py:616
  15.3 1.8 collective-permute-start.2
  15.7 49.3 %copy-start.22 = (bf16[128,1664]{1,0:T(8,128)(2,1)}, bf16[128,1664]{1,0:T(8,128)(2,1)S(1)}, u32[]{:S(2)}) copy-start(bf16[128,1664]{1,0:T(8,128)(2,1)S(1)} %fusion.4.refs_0_) | copy-start | bytes 1277956
  17.1 47.9 %collective-permute-start.4 = (bf16[128,1664]{1,0:T(8,128)(2,1)S(1)}, bf16[128,1664]{1,0:T(8,128)(2,1)S(1)}, u32[]{:S(2)}, u32[]{:S(2)}) collective-permute-start(bf16[128,1664]{1,0:T(8,128)(2,1)S(1)} %fusion.4.refs_0_), channel_id=1, source_target_pairs={{0,2},{1,3},{2,0},{3,1},{4,6},{5,7},{6,4},{7,5},{8,10},{9,11},{10,... | collective-permute-start | bytes 1277960 | tf_op jit(solution)/shard_map/ppermute | solution.py:616
  17.5 47.8 %collective-permute-start.3 = (bf16[128,1664]{1,0:T(8,128)(2,1)S(1)}, bf16[128,1664]{1,0:T(8,128)(2,1)}, u32[]{:S(2)}, u32[]{:S(2)}) collective-permute-start(bf16[128,1664]{1,0:T(8,128)(2,1)S(1)} %fusion.4.refs_0_), channel_id=1, source_target_pairs={{0,1},{1,0},{2,3},{3,2},{4,5},{5,4},{6,7},{7,6},{8,9},{9,8},{10,11... | collective-permute-start | bytes 1277960 | tf_op jit(solution)/shard_map/ppermute | solution.py:616
  17.8 47.3 %copy-start.31 = (s32[1,4]{1,0:T(1,128)S(1)}, s32[1,4]{1,0:T(1,128)}, u32[]{:S(2)}) copy-start(s32[1,4]{1,0:T(1,128)} %param.26) | copy-start | bytes 52
  65.0 1.8 collective-permute-start.5
  92.9 2.9 %collective-permute-start.6 = (bf16[2,128,1536]{2,1,0:T(8,128)(2,1)}, bf16[2,128,1536]{2,1,0:T(8,128)(2,1)S(1)}, u32[]{:S(2)}, u32[]{:S(2)}) collective-permute-start(bf16[2,128,1536]{2,1,0:T(8,128)(2,1)} %dynamic-slice_bitcast_fusion), channel_id=1, source_target_pairs={{0,1},{1,0},{2,3},{3,2},{4,5},{5,4},{6,7},{7,6},{8,9},{9,8},{10,11... | collective-permute-start | bytes 2359304 | tf_op jit(solution)/shard_map/ppermute | solution.py:616
  96.1 20.7 %collective-permute-start.7 = (bf16[1,128,1536]{2,1,0:T(8,128)(2,1)S(1)}, bf16[1,128,1536]{2,1,0:T(8,128)(2,1)S(1)}, u32[]{:S(2)}, u32[]{:S(2)}) collective-permute-start(bf16[1,128,1536]{2,1,0:T(8,128)(2,1)S(1)} %constant_dynamic-slice_fusion.3), channel_id=1, source_target_pairs={{0,2},{1,3},{2,0},{3,1},{4,6},{5,7},{6,4},{7,5},{8,10},{9,11},{10,... | collective-permute-start | bytes 1179656 | tf_op jit(solution)/shard_map/ppermute | solution.py:616
  97.9 18.9 %collective-permute-start.8 = (f32[32,512]{1,0:T(8,128)S(1)}, f32[32,512]{1,0:T(8,128)S(1)}, u32[]{:S(2)}, u32[]{:S(2)}) collective-permute-start(f32[32,512]{1,0:T(8,128)S(1)} %pad_maximum_fusion.3), channel_id=1, source_target_pairs={{0,1},{1,0},{2,3},{3,2},{4,5},{5,4},{6,7},{7,6},{8,9},{9,8},{10,11... | collective-permute-start | bytes 196616 | tf_op jit(solution)/shard_map/ppermute | solution.py:616
  117.0 27.9 %collective-permute-start.9 = (bf16[128,1536]{1,0:T(8,128)(2,1)S(1)}, bf16[128,1536]{1,0:T(8,128)(2,1)S(1)}, u32[]{:S(2)}, u32[]{:S(2)}) collective-permute-start(bf16[128,1536]{1,0:T(8,128)(2,1)S(1)} %fusion.5), channel_id=1, source_target_pairs={{0,4},{4,0},{8,12},{12,8},{16,20},{20,16},{24,28},{28,24},{1,5},{5... | collective-permute-start | bytes 1179656 | tf_op jit(solution)/shard_map/ppermute | solution.py:616
  117.0 27.8 %collective-permute-start.10 = (f32[32,512]{1,0:T(8,128)S(1)}, f32[32,512]{1,0:T(8,128)S(1)}, u32[]{:S(2)}, u32[]{:S(2)}) collective-permute-start(f32[32,512]{1,0:T(8,128)S(1)} %add.91), channel_id=1, source_target_pairs={{0,2},{1,3},{2,0},{3,1},{4,6},{5,7},{6,4},{7,5},{8,10},{9,11},{10,... | collective-permute-start | bytes 196616 | tf_op jit(solution)/shard_map/ppermute | solution.py:616
  146.1 20.9 %collective-permute-start.11 = (bf16[128,1536]{1,0:T(8,128)(2,1)S(1)}, bf16[128,1536]{1,0:T(8,128)(2,1)S(1)}, u32[]{:S(2)}, u32[]{:S(2)}) collective-permute-start(bf16[128,1536]{1,0:T(8,128)(2,1)S(1)} %add_convert_fusion.2), channel_id=1, source_target_pairs={{0,8},{4,12},{8,0},{12,4},{16,24},{20,28},{24,16},{28,20},{1,9},{5... | collective-permute-start | bytes 1179656 | tf_op jit(solution)/shard_map/ppermute | solution.py:616
  146.2 20.8 %collective-permute-start.13 = (bf16[2,128,768]{2,1,0:T(8,128)(2,1)S(1)}, bf16[2,128,768]{2,1,0:T(8,128)(2,1)S(1)}, u32[]{:S(2)}, u32[]{:S(2)}) collective-permute-start(bf16[2,128,768]{2,1,0:T(8,128)(2,1)S(1)} %dynamic-slice_bitcast_fusion.2), channel_id=1, source_target_pairs={{0,1},{1,0},{2,3},{3,2},{4,5},{5,4},{6,7},{7,6},{8,9},{9,8},{10,11... | collective-permute-start | bytes 1179656 | tf_op jit(solution)/shard_map/ppermute | solution.py:616
  146.2 20.7 %collective-permute-start.12 = (f32[32,512]{1,0:T(8,128)S(1)}, f32[32,512]{1,0:T(8,128)S(1)}, u32[]{:S(2)}, u32[]{:S(2)}) collective-permute-start(f32[32,512]{1,0:T(8,128)S(1)} %add.93), channel_id=1, source_target_pairs={{0,4},{4,0},{8,12},{12,8},{16,20},{20,16},{24,28},{28,24},{1,5},{5... | collective-permute-start | bytes 196616 | tf_op jit(solution)/shard_map/ppermute | solution.py:616
  167.3 28.1 %collective-permute-start.14 = (bf16[128,1536]{1,0:T(8,128)(2,1)S(1)}, bf16[128,1536]{1,0:T(8,128)(2,1)S(1)}, u32[]{:S(2)}, u32[]{:S(2)}) collective-permute-start(bf16[128,1536]{1,0:T(8,128)(2,1)S(1)} %add_convert_fusion.1), channel_id=1, source_target_pairs={{0,16},{4,20},{8,24},{12,28},{16,0},{20,4},{24,8},{28,12},{1,17},{... | collective-permute-start | bytes 1179656 | tf_op jit(solution)/shard_map/ppermute | solution.py:616
  174.7 20.7 %collective-permute-start.16 = (bf16[1,128,768]{2,1,0:T(8,128)(2,1)S(1)}, bf16[1,128,768]{2,1,0:T(8,128)(2,1)S(1)}, u32[]{:S(2)}, u32[]{:S(2)}) collective-permute-start(bf16[1,128,768]{2,1,0:T(8,128)(2,1)S(1)} %constant_dynamic-slice_fusion.2), channel_id=1, source_target_pairs={{0,2},{1,3},{2,0},{3,1},{4,6},{5,7},{6,4},{7,5},{8,10},{9,11},{10,... | collective-permute-start | bytes 589832 | tf_op jit(solution)/shard_map/ppermute | solution.py:616
  175.2 20.2 %collective-permute-start.15 = (f32[32,512]{1,0:T(8,128)S(1)}, f32[32,512]{1,0:T(8,128)S(1)}, u32[]{:S(2)}, u32[]{:S(2)}) collective-permute-start(f32[32,512]{1,0:T(8,128)S(1)} %add.95), channel_id=1, source_target_pairs={{0,8},{4,12},{8,0},{12,4},{16,24},{20,28},{24,16},{28,20},{1,9},{5... | collective-permute-start | bytes 196616 | tf_op jit(solution)/shard_map/ppermute | solution.py:616
  196.7 2.2 collective-permute-start.17
  199.1 16.8 %collective-permute-start.18 = (bf16[1,128,768]{2,1,0:T(8,128)(2,1)S(1)}, bf16[1,128,768]{2,1,0:T(8,128)(2,1)S(1)}, u32[]{:S(2)}, u32[]{:S(2)}) collective-permute-start(bf16[1,128,768]{2,1,0:T(8,128)(2,1)S(1)} %constant_dynamic-slice_fusion.1), channel_id=1, source_target_pairs={{0,2},{1,3},{2,0},{3,1},{4,6},{5,7},{6,4},{7,5},{8,10},{9,11},{10,... | collective-permute-start | bytes 589832 | tf_op jit(solution)/shard_map/ppermute | solution.py:616
  204.4 11.4 %collective-permute-start.19 = (f32[32,512]{1,0:T(8,128)S(1)}, f32[32,512]{1,0:T(8,128)S(1)}, u32[]{:S(2)}, u32[]{:S(2)}) collective-permute-start(f32[32,512]{1,0:T(8,128)S(1)} %add.99), channel_id=1, source_target_pairs={{0,16},{4,20},{8,24},{12,28},{16,0},{20,4},{24,8},{28,12},{1,17},{... | collective-permute-start | bytes 196616 | tf_op jit(solution)/shard_map/ppermute | solution.py:616
  215.8 32.3 %copy-start = (f32[128,1536]{1,0:T(8,128)S(1)}, f32[128,1536]{1,0:T(8,128)}, u32[]{:S(2)}) copy-start(f32[128,1536]{1,0:T(8,128)} %refs_0_.5) | copy-start | bytes 2359300
  233.7 14.4 %all-to-all-start.1 = ((bf16[8,16,1536]{2,1,0:T(8,128)(2,1)}), bf16[8,16,1536]{2,1,0:T(8,128)(2,1)S(1)}, u32[]{:S(2)}, u32[]{:S(2)}) async-start(bf16[8,16,1536]{2,1,0:T(8,128)(2,1)} %tile.2), calls=%async_computation.1 | async-start | bytes 786432 | tf_op jit(solution)/shard_map/all_to_all | solution.py:710
  (31 other events, 249.3 us)
